TPU v7x, 512 devices: a whole 4x8x8 slice. The times are simulated.
512 devices in a mesh: wide: 64 (over y, x, core), tall: 8 (over z).
Axes of the slice: x: 4, y: 8, z: 8, core: 2. Of those that a mesh axis runs over, the one named last changes fastest.
Arguments:
- tokens: bfloat16 [192, 1536, 512], P('tall', 'wide'), may hold values from -6 to 6
- qkv_weight: bfloat16 [512, 1536], replicated, may hold values from -0.25 to 0.25
- proj_weight: bfloat16 [512, 512], replicated, may hold values from -0.25 to 0.25
- head_scale: float32 [16], replicated, may hold values from 5 to 100
- attn_gain: float32 [512], replicated, may hold values from 0.5 to 1.5
- router: bfloat16 [512, 64], replicated, may hold values from -0.25 to 0.25
- expert_in: bfloat16 [64, 512, 2048], P('wide', None, 'tall'), may hold values from -0.25 to 0.25
- expert_out: bfloat16 [64, 2048, 512], P('wide', 'tall'), may hold values from -0.125 to 0.125
- moe_gain: float32 [512], replicated, may hold values from 0.5 to 1.5
- expert_ids: int32 [8, 64, 576, 1], P('tall', 'wide'), may hold values from 0 to 63; in each aligned block of 576 rows (0 to 575, 576 to 1151, ..., all dimensions but the last counted through in order) at most 13 rows name the same one
- keep: int32 [8, 64, 576], P('tall', 'wide'), may hold values 0 or 1
Outputs:
- mixed: bfloat16 [192, 1536, 512], P('tall', 'wide')
Inputs may be any that keep to these rules, and one draw needn't show every extreme that they name: `expert_ids`: within the tokens of one tile (one index of the first two dimensions), no expert is named more than 13 times, a bound that some block reaches.
All inputs are finite; a program needn't handle non-finite values. No bound on the sum of `keep` on one device may be relied on, other than what follows from the above.
Results may differ from a plain program's by a relative error of at most 0.012.
The roundings to bfloat16 on the way count: a program that leaves them out, or rounds other values in their place, can miss the bound.
Values may be sent and summed in bfloat16 or wider, within the bound.
A program may use at most 64 MiB of HBM per device.

v0:
```python
import math

import jax
import jax.numpy as jnp
from jax import lax
from jax.sharding import PartitionSpec as P


def shifted(value, axis, by):
    peers = lax.axis_size(axis)
    return lax.ppermute(value, axis, [(i, (i + by) % peers) for i in range(peers)])


def normalize(values_in, gain_vec):
    average = jnp.mean(values_in, axis=-1, keepdims=True)
    centered = values_in - average
    spread = jnp.mean(centered * centered, axis=-1, keepdims=True)
    return centered * lax.rsqrt(spread + 1e-05) * gain_vec


def unit_heads(block, head_count):
    shaped = block.reshape(block.shape[0], head_count, -1).transpose(1, 0, 2)
    return (shaped * lax.rsqrt(jnp.sum(shaped * shaped, axis=-1, keepdims=True) + 1e-06)).astype(
        jnp.bfloat16
    )


def window_attention(
    window,
    first_row,
    first_col,
    window_edge,
    shift_cells,
    total_rows,
    total_cols,
    qkv_weight,
    proj_weight,
    head_scale,
):
    window_len, feature = window.shape
    head_count = head_scale.shape[0]
    head_size = feature // head_count
    offsets = jnp.arange(window_len, dtype=jnp.int32)
    row_index = first_row + offsets // window_edge
    col_index = first_col + offsets % window_edge
    region = (row_index + shift_cells >= total_rows).astype(jnp.int32) * 2 + (
        col_index + shift_cells >= total_cols
    ).astype(jnp.int32)
    masking = jnp.where(region[:, None] == region[None, :], 0.0, -100.0).astype(jnp.float32)
    project = jnp.dot(window, qkv_weight, preferred_element_type=jnp.float32)
    queries = unit_heads(project[:, :feature], head_count)
    key_heads = unit_heads(project[:, feature : 2 * feature], head_count)
    value_heads = (
        project[:, 2 * feature :]
        .astype(jnp.bfloat16)
        .reshape(window_len, head_count, head_size)
        .transpose(1, 0, 2)
    )
    group_size = math.gcd(4, head_count)

    def one_group(pieces):
        query_part, key_part, value_part, scale_part = pieces
        scores = jnp.einsum(
            "hqd,hkd->hqk", query_part, key_part, preferred_element_type=jnp.float32
        )
        scores = scores * scale_part[:, None, None] + masking[None]
        weights_soft = jax.nn.softmax(scores, axis=-1).astype(jnp.bfloat16)
        return jnp.einsum(
            "hqk,hkd->hqd", weights_soft, value_part, preferred_element_type=jnp.float32
        ).astype(jnp.bfloat16)

    def grouped(array_in):
        return array_in.reshape((head_count // group_size, group_size) + array_in.shape[1:])

    attended = lax.map(
        one_group, (grouped(queries), grouped(key_heads), grouped(value_heads), grouped(head_scale))
    )
    attended = (
        attended.reshape(head_count, window_len, head_size)
        .transpose(1, 0, 2)
        .reshape(window_len, feature)
    )
    return jnp.dot(attended, proj_weight, preferred_element_type=jnp.float32)


def body(
    tokens,
    qkv_weight,
    proj_weight,
    head_scale,
    attn_gain,
    router,
    expert_in,
    expert_out,
    moe_gain,
    expert_ids,
    keep,
):
    tile_rows, window_edge, feature = tokens.shape
    shift_cells = window_edge // 2
    full_in = lax.all_gather(expert_in, "tall", axis=2, tiled=True)[0]
    full_out = lax.all_gather(expert_out, "tall", axis=1, tiled=True)[0]
    lower_part = shifted(tokens[:shift_cells], "tall", -1)
    heightened = jnp.concatenate([tokens[shift_cells:], lower_part], axis=0)
    right_part = shifted(heightened[:, :shift_cells], "wide", -1)
    rolled = jnp.concatenate([heightened[:, shift_cells:], right_part], axis=1)
    total_rows = tile_rows * lax.axis_size("tall")
    total_cols = window_edge * lax.axis_size("wide")
    first_row = lax.axis_index("tall") * tile_rows
    first_col = lax.axis_index("wide") * window_edge
    window_count = tile_rows // window_edge
    windows = rolled.reshape(window_count, window_edge * window_edge, feature)
    starts = first_row + jnp.arange(window_count, dtype=jnp.int32) * window_edge

    def per_window(pieces):
        window, start_row = pieces
        attended = window_attention(
            window,
            start_row,
            first_col,
            window_edge,
            shift_cells,
            total_rows,
            total_cols,
            qkv_weight,
            proj_weight,
            head_scale,
        )
        return (window.astype(jnp.float32) + normalize(attended, attn_gain)).astype(jnp.bfloat16)

    mixed_in = lax.map(per_window, (windows, starts)).reshape(-1, feature)
    route_ids = expert_ids[0, 0, :, 0]
    keep_flag = keep[0, 0]
    experts = router.shape[1]
    tokens_here = route_ids.shape[0]
    capacity = max(2, 3 * tokens_here // (2 * experts))
    onehot = (route_ids[:, None] == jnp.arange(experts, dtype=jnp.int32)[None, :]).astype(jnp.int32)
    live_hits = onehot * keep_flag[:, None]
    before = jnp.cumsum(live_hits, axis=0) - live_hits
    slot_ids = jnp.sum(before * onehot, axis=1)
    target = jnp.where(keep_flag == 1, route_ids * capacity + slot_ids, experts * capacity)
    outgoing = jnp.zeros((experts * capacity + 1, feature), jnp.bfloat16).at[target].set(mixed_in)
    outgoing = outgoing[: experts * capacity].reshape(experts, capacity, feature)
    arrived = lax.all_to_all(outgoing, "wide", split_axis=0, concat_axis=0, tiled=True).reshape(
        -1, feature
    )
    hidden = jax.nn.gelu(
        jnp.dot(arrived, full_in, preferred_element_type=jnp.float32), approximate=False
    ).astype(jnp.bfloat16)
    produced = jnp.dot(hidden, full_out, preferred_element_type=jnp.float32)
    returned = lax.all_to_all(
        produced.astype(jnp.bfloat16).reshape(experts, capacity, feature),
        "wide",
        split_axis=0,
        concat_axis=0,
        tiled=True,
    )
    padded_back = jnp.concatenate(
        [returned.reshape(-1, feature), jnp.zeros((1, feature), jnp.bfloat16)], axis=0
    )
    picked = padded_back[target]
    logits = jnp.dot(mixed_in, router, preferred_element_type=jnp.float32)
    gate_prob = jax.nn.sigmoid(jnp.sum(logits * onehot.astype(jnp.float32), axis=1))
    scaled = keep_flag.astype(jnp.float32) * gate_prob
    result_rows = (
        mixed_in.astype(jnp.float32)
        + scaled[:, None] * normalize(picked.astype(jnp.float32), moe_gain)
    ).astype(jnp.bfloat16)
    return result_rows.reshape(tile_rows, window_edge, feature)


def solution(mesh):
    placed = (
        P("tall", "wide", None),
        P(),
        P(),
        P(),
        P(),
        P(),
        P("wide", None, "tall"),
        P("wide", "tall", None),
        P(),
        P("tall", "wide", None, None),
        P("tall", "wide", None),
    )
    return jax.shard_map(
        body, mesh=mesh, in_specs=placed, out_specs=P("tall", "wide", None), check_vma=False
    )
```

profile of v0, /device:TPU:1, one launch (start us, length us, event | category | flops | bytes accessed | tf_op | source)
XLA Modules:
  0.0 207.7 jit_solution(8245183336943197049)
XLA Ops:
  6.5 0.7 all-gather.3.cloned.1.call-update
  7.3 0.0 all-gather.5.cloned.1.call-start
  7.3 1.1 fusion.131
  8.4 11.5 %collective-permute-start = (bf16[12,24,512]{2,1,0:T(8,128)(2,1)S(1)}, bf16[12,24,512]{2,1,0:T(8,128)(2,1)S(1)}, u32[]{:S(2)}, u32[]{:S(2)}) collective-permute-start(bf16[12,24,512]{2,1,0:T(8,128)(2,1)S(1)} %get-tuple-element.108), channel_id=1, source_target_pairs={{0,7},{1,0},{2,1},{3,2},{4,3},{5,4},{6,5},{7,6},{8,15},{9,8},{10,9... | collective-permute-start | bytes 884744 | tf_op jit(solution)/shard_map/ppermute | solution.py:11
  19.9 0.0 all-gather.5.cloned.1.call-update
  19.9 0.7 reshape.223
  20.7 0.7 reduce
  21.4 0.7 reduce.1
  22.1 1.5 reduce-window.6
  23.6 0.3 slice_reduce_fusion
  23.9 0.1 bitcast_bitcast_fusion
  24.1 1.5 collective-permute-done
  25.6 0.1 fusion.73
  25.7 3.5 %collective-permute-start.1 = (bf16[24,12,512]{2,1,0:T(8,128)(2,1)S(1)}, bf16[24,12,512]{2,1,0:T(8,128)(2,1)S(1)}, u32[]{:S(2)}, u32[]{:S(2)}) collective-permute-start(bf16[24,12,512]{2,1,0:T(8,128)(2,1)S(1)} %get-tuple-element.106), channel_id=1, source_target_pairs={{0,504},{8,0},{16,8},{24,16},{32,24},{40,32},{48,40},{56,48},{64,5... | collective-permute-start | bytes 884744 | tf_op jit(solution)/shard_map/ppermute | solution.py:11
  29.2 0.7 fusion.90
  30.0 6.1 %collective-permute-done.1 = bf16[24,12,512]{2,1,0:T(8,128)(2,1)S(1)} collective-permute-done((bf16[24,12,512]{2,1,0:T(8,128)(2,1)S(1)}, bf16[24,12,512]{2,1,0:T(8,128)(2,1)S(1)}, u32[]{:S(2)}, u32[]{:S(2)}) %collective-permute-start.1) | collective-permute-done | bytes 294944 | tf_op jit(solution)/shard_map/ppermute | solution.py:11
  36.1 0.2 pad_maximum_fusion
  36.3 0.8 copy-done.1
  37.1 1.1 fusion.133
  38.2 1.6 fusion.130
  39.8 0.1 slice.71
  39.9 1.7 copy.19
  41.5 0.2 multiply_reduce_fusion
  41.7 1.0 multiply_convert_fusion
  42.7 1.7 copy.18
  44.4 0.2 multiply_reduce_fusion.1
  44.6 0.9 multiply_convert_fusion.1
  45.5 1.1 copy.20
  46.6 39.0 %while.18 = (s32[]{:T(128)}, bf16[4,4,576,32]{2,3,1,0:T(8,128)(2,1)}, bf16[4,4,576,32]{2,3,1,0:T(8,128)(2,1)}, bf16[4,4,576,32]{2,3,1,0:T(8,128)(2,1)}, f32[4,4]...) while((s32[]{:T(128)}, bf16[4,4,576,32]{2,3,1,0:T(8,128)(2,1)}, ...), condition=%wide.region_5.6_spmd.clone, body=%wide.region_2.5_spmd.clone.sunk | while | flops 178569792 | bytes 14539145 | solution.py:75
  46.6 0.2 compare_select_fusion.3
  46.8 5.5 %fusion.151 = (f32[4,576]{1,0:T(4,128)S(1)}, f32[4,576,576]{1,2,0:T(8,128)}) fusion(f32[576,576]{0,1:T(8,128)S(1)} %compare_select_fusion.3, f32[4]{0:T(128)S(1)} %fusion.150, bf16[4,4,576,32]{2,3,1,0:T(8,128)(2,1)} %get-tuple-element.177, s32[]{:T(128)} %get-tuple-element.166, bf16[4,4,576,32]{2,3,1,0:T(8,128)(2,1)} %get-tuple-element.176), kind=kOutput, calls=%fused_computation.152.clone.1 | convolution fusion | flops 90243648 | bytes 6973456 | tf_op jit(solution)/shard_map/while/body/eval_jaxpr/while/body/eval_jaxpr/sub | solution.py:67
  52.3 4.1 %fusion.152 = bf16[4,4,576,32]{2,3,1,0:T(8,128)(2,1)} fusion(bf16[4,4,576,32]{2,3,1,0:T(8,128)(2,1)} %get-tuple-element.167, s32[]{:T(128)} %get-tuple-element.166, f32[4,576,576]{1,2,0:T(8,128)} %get-tuple-element.156, f32[4,576]{1,0:T(4,128)S(1)} %get-tuple-element.157, bf16[4,4,576,32]{2,3,1,0:T(8,128)(2,1)} %get-tuple-element.179), kind=kOutput, calls=%fused_computation.14.clone.1 | convolution fusion | flops 87662592 | bytes 6236160 | tf_op jit(solution)/shard_map/while/body/eval_jaxpr/while/body/eval_jaxpr/hqk,hkd->hqd/dot_general | solution.py:68
  56.4 0.2 compare_select_fusion.3
  56.6 5.5 %fusion.151 = (f32[4,576]{1,0:T(4,128)S(1)}, f32[4,576,576]{1,2,0:T(8,128)}) fusion(f32[576,576]{0,1:T(8,128)S(1)} %compare_select_fusion.3, f32[4]{0:T(128)S(1)} %fusion.150, bf16[4,4,576,32]{2,3,1,0:T(8,128)(2,1)} %get-tuple-element.177, s32[]{:T(128)} %get-tuple-element.166, bf16[4,4,576,32]{2,3,1,0:T(8,128)(2,1)} %get-tuple-element.176), kind=kOutput, calls=%fused_computation.152.clone.1 | convolution fusion | flops 90243648 | bytes 6973456 | tf_op jit(solution)/shard_map/while/body/eval_jaxpr/while/body/eval_jaxpr/sub | solution.py:67
  62.1 4.0 %fusion.152 = bf16[4,4,576,32]{2,3,1,0:T(8,128)(2,1)} fusion(bf16[4,4,576,32]{2,3,1,0:T(8,128)(2,1)} %get-tuple-element.167, s32[]{:T(128)} %get-tuple-element.166, f32[4,576,576]{1,2,0:T(8,128)} %get-tuple-element.156, f32[4,576]{1,0:T(4,128)S(1)} %get-tuple-element.157, bf16[4,4,576,32]{2,3,1,0:T(8,128)(2,1)} %get-tuple-element.179), kind=kOutput, calls=%fused_computation.14.clone.1 | convolution fusion | flops 87662592 | bytes 6236160 | tf_op jit(solution)/shard_map/while/body/eval_jaxpr/while/body/eval_jaxpr/hqk,hkd->hqd/dot_general | solution.py:68
  66.1 0.2 compare_select_fusion.3
  66.3 5.5 %fusion.151 = (f32[4,576]{1,0:T(4,128)S(1)}, f32[4,576,576]{1,2,0:T(8,128)}) fusion(f32[576,576]{0,1:T(8,128)S(1)} %compare_select_fusion.3, f32[4]{0:T(128)S(1)} %fusion.150, bf16[4,4,576,32]{2,3,1,0:T(8,128)(2,1)} %get-tuple-element.177, s32[]{:T(128)} %get-tuple-element.166, bf16[4,4,576,32]{2,3,1,0:T(8,128)(2,1)} %get-tuple-element.176), kind=kOutput, calls=%fused_computation.152.clone.1 | convolution fusion | flops 90243648 | bytes 6973456 | tf_op jit(solution)/shard_map/while/body/eval_jaxpr/while/body/eval_jaxpr/sub | solution.py:67
  71.8 4.0 %fusion.152 = bf16[4,4,576,32]{2,3,1,0:T(8,128)(2,1)} fusion(bf16[4,4,576,32]{2,3,1,0:T(8,128)(2,1)} %get-tuple-element.167, s32[]{:T(128)} %get-tuple-element.166, f32[4,576,576]{1,2,0:T(8,128)} %get-tuple-element.156, f32[4,576]{1,0:T(4,128)S(1)} %get-tuple-element.157, bf16[4,4,576,32]{2,3,1,0:T(8,128)(2,1)} %get-tuple-element.179), kind=kOutput, calls=%fused_computation.14.clone.1 | convolution fusion | flops 87662592 | bytes 6236160 | tf_op jit(solution)/shard_map/while/body/eval_jaxpr/while/body/eval_jaxpr/hqk,hkd->hqd/dot_general | solution.py:68
  75.9 0.2 compare_select_fusion.3
  76.1 5.5 %fusion.151 = (f32[4,576]{1,0:T(4,128)S(1)}, f32[4,576,576]{1,2,0:T(8,128)}) fusion(f32[576,576]{0,1:T(8,128)S(1)} %compare_select_fusion.3, f32[4]{0:T(128)S(1)} %fusion.150, bf16[4,4,576,32]{2,3,1,0:T(8,128)(2,1)} %get-tuple-element.177, s32[]{:T(128)} %get-tuple-element.166, bf16[4,4,576,32]{2,3,1,0:T(8,128)(2,1)} %get-tuple-element.176), kind=kOutput, calls=%fused_computation.152.clone.1 | convolution fusion | flops 90243648 | bytes 6973456 | tf_op jit(solution)/shard_map/while/body/eval_jaxpr/while/body/eval_jaxpr/sub | solution.py:67
  81.6 4.0 %fusion.152 = bf16[4,4,576,32]{2,3,1,0:T(8,128)(2,1)} fusion(bf16[4,4,576,32]{2,3,1,0:T(8,128)(2,1)} %get-tuple-element.167, s32[]{:T(128)} %get-tuple-element.166, f32[4,576,576]{1,2,0:T(8,128)} %get-tuple-element.156, f32[4,576]{1,0:T(4,128)S(1)} %get-tuple-element.157, bf16[4,4,576,32]{2,3,1,0:T(8,128)(2,1)} %get-tuple-element.179), kind=kOutput, calls=%fused_computation.14.clone.1 | convolution fusion | flops 87662592 | bytes 6236160 | tf_op jit(solution)/shard_map/while/body/eval_jaxpr/while/body/eval_jaxpr/hqk,hkd->hqd/dot_general | solution.py:68
  85.6 1.8 fusion.132
  87.5 0.3 multiply_reduce_fusion.2
  87.8 1.4 add_convert_fusion
  89.1 0.0 copy-start.2
  89.2 0.8 copy-done.2
  90.0 6.0 %scatter_custom_fusion = bf16[833,512]{1,0:T(8,128)(2,1)S(1)} fusion(s32[576]{0:T(1024)S(1)} %fusion.90, bf16[576,512]{1,0:T(8,128)(2,1)S(1)} %add_convert_fusion, bf16[]{:T(256)} %constant.60.clone.1), kind=kCustom, calls=%fused_computation.77 | custom fusion | bytes 852994 | tf_op jit(solution)/shard_map/scatter | solution.py:142
  95.9 0.1 slice.57
  96.0 0.3 reshape.230
  96.3 38.6 %all_to_all.10 = bf16[64,13,512]{2,1,0:T(8,128)(2,1)} all-to-all(bf16[64,13,512]{2,1,0:T(8,128)(2,1)S(1)} %reshape.230), channel_id=1, replica_groups=mesh['wide'=64,'tall'=8] {'wide'}, dimensions={0} | all-to-all | bytes 1703936 | tf_op jit(solution)/shard_map/all_to_all | solution.py:144
  134.9 1.6 reshape.231
  136.5 0.0 all-gather.3.cloned.1.call-done
  136.5 0.0 all-gather.5.cloned.1.call-done
  136.6 19.6 %fusion.56 = bf16[832,512]{1,0:T(8,128)(2,1)} fusion(bf16[1,2048,512]{2,1,0:T(8,128)(2,1)} %all-gather.5.cloned.1.call-done, bf16[832,512]{1,0:T(8,128)(2,1)S(1)} %reshape.231, bf16[1,512,2048]{2,1,0:T(8,128)(2,1)} %all-gather.3.cloned.1.call-done), kind=kOutput, calls=%fused_computation.57 | convolution fusion | flops 3600842752 | bytes 5898240 | tf_op jit(solution)/shard_map/dot_general | solution.py:150
  156.2 2.2 %reshape.232 = bf16[64,13,512]{2,1,0:T(8,128)(2,1)} reshape(bf16[832,512]{1,0:T(8,128)(2,1)} %fusion.56) | data formatting | bytes 1703936 | tf_op jit(solution)/shard_map/reshape | solution.py:152
  158.4 6.5 %all-to-all-start.1 = ((bf16[64,13,512]{2,1,0:T(8,128)(2,1)}), bf16[64,13,512]{2,1,0:T(8,128)(2,1)S(1)}, u32[]{:S(2)}, u32[]{:S(2)}) async-start(bf16[64,13,512]{2,1,0:T(8,128)(2,1)} %reshape.232), calls=%async_computation.1 | async-start | bytes 2097152 | tf_op jit(solution)/shard_map/all_to_all | solution.py:151
  165.0 0.3 fusion.70
  165.3 27.6 %all-to-all-done.1 = bf16[64,13,512]{2,1,0:T(8,128)(2,1)S(1)} async-done(((bf16[64,13,512]{2,1,0:T(8,128)(2,1)}), bf16[64,13,512]{2,1,0:T(8,128)(2,1)S(1)}, u32[]{:S(2)}, u32[]{:S(2)}) %all-to-all-start.1) | async-done | bytes 852000 | tf_op jit(solution)/shard_map/all_to_all | solution.py:151
  192.9 1.2 reshape.233
  194.1 1.2 concatenate.11
  195.3 2.7 %gather_fusion = bf16[576,512]{1,0:T(8,128)(2,1)S(1)} fusion(bf16[833,512]{1,0:T(8,128)(2,1)S(1)} %concatenate.11, s32[1024]{0:T(1024)S(1)} %pad_clamp_fusion), kind=kCustom, calls=%fused_computation | custom fusion | bytes 1181952 | tf_op jit(solution)/shard_map/gather | solution.py:161
  198.1 0.2 convert_reduce_fusion
  198.3 0.3 fusion.65
  198.6 2.3 %fusion.69 = bf16[576,512]{1,0:T(8,128)(2,1)} fusion(bf16[576,512]{1,0:T(8,128)(2,1)S(1)} %gather_fusion, bf16[576,512]{1,0:T(8,128)(2,1)} %copy-done.2, f32[512]{0:T(512)S(1)} %copy-done.5, f32[576]{0:T(1024)S(1)} %add_rsqrt_fusion.2, f32[576]{0:T(1024)S(1)} %broadcast_multiply_fusion, f32[576]{0:T(1024)S(1)} %divide_multiply_fusion), kind=kLoop, calls=%fused_computation.68 | loop fusion | flops 2359296 | bytes 1778432 | tf_op jit(solution)/shard_map/convert_element_type | solution.py:168
  (30 shorter events, 0.2 us)
Async XLA Ops:
  6.5 30.5 %copy-start = (bf16[512,1536]{1,0:T(8,128)(2,1)S(1)}, bf16[512,1536]{1,0:T(8,128)(2,1)}, u32[]{:S(2)}) copy-start(bf16[512,1536]{1,0:T(8,128)(2,1)} %param.14) | copy-start | bytes 4718596
  6.5 130.0 %all-gather.3.cloned.1.call-start = ((), (), s32[]{:S(2)}) async-start(), calls=%async_computation.2 | async-start | bytes 2359296 | tf_op jit(solution)/shard_map/all_gather | solution.py:101
  7.3 129.3 %all-gather.5.cloned.1.call-start = ((), (), s32[]{:S(2)}) async-start(), calls=%async_computation.3 | async-start | bytes 2359296 | tf_op jit(solution)/shard_map/all_gather | solution.py:102
  8.4 17.2 %collective-permute-start = (bf16[12,24,512]{2,1,0:T(8,128)(2,1)S(1)}, bf16[12,24,512]{2,1,0:T(8,128)(2,1)S(1)}, u32[]{:S(2)}, u32[]{:S(2)}) collective-permute-start(bf16[12,24,512]{2,1,0:T(8,128)(2,1)S(1)} %get-tuple-element.108), channel_id=1, source_target_pairs={{0,7},{1,0},{2,1},{3,2},{4,3},{5,4},{6,5},{7,6},{8,15},{9,8},{10,9... | collective-permute-start | bytes 884744 | tf_op jit(solution)/shard_map/ppermute | solution.py:11
  25.7 10.4 %collective-permute-start.1 = (bf16[24,12,512]{2,1,0:T(8,128)(2,1)S(1)}, bf16[24,12,512]{2,1,0:T(8,128)(2,1)S(1)}, u32[]{:S(2)}, u32[]{:S(2)}) collective-permute-start(bf16[24,12,512]{2,1,0:T(8,128)(2,1)S(1)} %get-tuple-element.106), channel_id=1, source_target_pairs={{0,504},{8,0},{16,8},{24,16},{32,24},{40,32},{48,40},{56,48},{64,5... | collective-permute-start | bytes 884744 | tf_op jit(solution)/shard_map/ppermute | solution.py:11
  36.3 0.8 copy-start.1
  46.6 41.2 %copy-start.4 = (f32[512]{0:T(512)S(1)}, f32[512]{0:T(512)}, u32[]{:S(2)}) copy-start(f32[512]{0:T(512)} %param.17) | copy-start | bytes 6148
  89.1 0.8 copy-start.2
  136.5 28.4 %copy-start.3 = (bf16[576,512]{1,0:T(8,128)(2,1)S(1)}, bf16[576,512]{1,0:T(8,128)(2,1)}, u32[]{:S(2)}) copy-start(bf16[576,512]{1,0:T(8,128)(2,1)} %copy-done.2) | copy-start | bytes 1769476
  136.5 28.4 %copy-start.6 = (bf16[512,64]{0,1:T(8,128)(2,1)S(1)}, bf16[512,64]{0,1:T(8,128)(2,1)}, u32[]{:S(2)}) copy-start(bf16[512,64]{0,1:T(8,128)(2,1)} %param.18) | copy-start | bytes 196612
  158.4 34.5 %all-to-all-start.1 = ((bf16[64,13,512]{2,1,0:T(8,128)(2,1)}), bf16[64,13,512]{2,1,0:T(8,128)(2,1)S(1)}, u32[]{:S(2)}, u32[]{:S(2)}) async-start(bf16[64,13,512]{2,1,0:T(8,128)(2,1)} %reshape.232), calls=%async_computation.1 | async-start | bytes 2097152 | tf_op jit(solution)/shard_map/all_to_all | solution.py:151
  164.9 33.7 %copy-start.5 = (f32[512]{0:T(512)S(1)}, f32[512]{0:T(512)}, u32[]{:S(2)}) copy-start(f32[512]{0:T(512)} %param.21) | copy-start | bytes 6148
Sparse Core Ops, SparseCore 0:
  9.4 52.4 all-gather.2
  63.9 43.0 all-gather.4
where the time goes:
time: 209 us; the launch traced here: 208 us
  matrix products  61.2 us (29%)
  blocking collectives  38.6 us (18%)
  waiting for transfers between devices  36 us (17%)
  local copies, waits for them, and re-layouts  25.2 us (12%)
  starting transfers between devices  21.4 us (10%)
  between operations  13.7 us (7%)
  other arithmetic  11.5 us (6%)
    all_to_all x1, blocking collectives, body(): lax.all_to_all(outgoing, 'wide', split_axis=0, concat_axis=0, tiled=True)  38.6 us
    all_to_all x1, waiting for transfers between devices, body(): lax.all_to_all(produced.astype(jnp.bfloat16).reshape(experts, capacity, f...  27.6 us
    sub x4, matrix products, one_group(): weights_soft = jax.nn.softmax(scores, axis=-1).astype(jnp.bfloat16)  22.1 us
    dot_general x1, matrix products, body(): produced = jnp.dot(hidden, full_out, preferred_element_type=jnp.float32)  19.6 us
    dot_general x4, matrix products, one_group(): jnp.einsum('hqk,hkd->hqd', weights_soft, value_part, preferred_element_ty...  16.2 us
    ppermute x2, starting transfers between devices, shifted(): lax.ppermute(value, axis, [(i, (i + by) % peers) for i in range(peers)])  15 us
    ppermute x2, waiting for transfers between devices, shifted(): lax.ppermute(value, axis, [(i, (i + by) % peers) for i in range(peers)])  7.65 us
    all_to_all x1, starting transfers between devices, body(): lax.all_to_all(produced.astype(jnp.bfloat16).reshape(experts, capacity, f...  6.46 us
  transfers between devices with their start and end apart: 5, of which 3 were waited for; matrix products, arithmetic and copies ran while one was open for 32% of the time, Pallas kernels for 0%

commit v1 on v0

v1 whole, which is shorter than its diff:
```python
import functools
import math

import jax
import jax.numpy as jnp
from jax import lax
from jax.experimental import pallas as pl
from jax.experimental.pallas import tpu as pltpu
from jax.sharding import PartitionSpec as P

F32, BF16, I32 = jnp.float32, jnp.bfloat16, jnp.int32
MESH = pl.DeviceIdType.MESH
EDGE = 24
HALF = EDGE // 2
TOK = EDGE * EDGE
QUAD = HALF * HALF
HEADS = 16
HEAD = 32
D = 512
GROUP = 4
SPAN = GROUP * TOK
TILE = 256
LOG2E = math.log2(math.e)
CENTRE = 0.375
SAFE = 2.0**-60
ROOM = 16
NT = (((1,), (1,)), ((), ()))
TN = (((0,), (0,)), ((), ()))
VMEM = pl.BlockSpec(memory_space=pltpu.VMEM)
SMEM = pl.BlockSpec(memory_space=pltpu.SMEM)
ANY = pl.BlockSpec(memory_space=pl.ANY)


def dot(a, b, dims=None):
    if dims is None:
        return jnp.dot(a, b, preferred_element_type=F32)
    return lax.dot_general(a, b, dims, preferred_element_type=F32)


def iota(shape, axis):
    return lax.broadcasted_iota(I32, shape, axis)


def norm(value, gain):
    mean = jnp.mean(value, axis=-1, keepdims=True)
    centred = value - mean
    return centred * lax.rsqrt(jnp.mean(centred * centred, axis=-1, keepdims=True) + 1e-5) * gain


def gelu(value):
    size = jnp.abs(value)
    t = 1.0 / (1.0 + (0.3275911 / math.sqrt(2.0)) * size)
    poly = t * (
        0.5 * 0.254829592
        + t * (0.5 * -0.284496736 + t * (0.5 * 1.421413741 + t * (0.5 * -1.453152027 + t * (0.5 * 1.061405429))))
    )
    return jnp.maximum(value, 0.0) - size * poly * jnp.exp2((-0.5 * LOG2E) * (value * value))


def unit(block):
    ones = (iota((TILE, TILE), 0) // HEAD == iota((TILE, TILE), 1) // HEAD).astype(BF16)
    square = block * block
    high = square.astype(BF16)
    low = (square - high.astype(F32)).astype(BF16)
    return (block * lax.rsqrt(dot(high, ones) + dot(low, ones) + 1e-6)).astype(BF16)


def region_column(total_rows, total_cols):
    place = iota((TOK, 1), 0)
    row = lax.axis_index("tall") * EDGE + place // EDGE
    col = lax.axis_index("wide") * EDGE + place % EDGE
    return (row + HALF >= total_rows).astype(I32) * 2 + (col + HALF >= total_cols).astype(I32)


def prepare(x, qkv_ref, scale_ref, region, q_ref, k_ref, v_ref):
    lane = iota((1, 128), 1)
    feat, own_head = lane % HEAD, lane // HEAD
    key_feat = jnp.where(feat < 12, jnp.where(region == feat % 4, 0.0, -1.0), jnp.where(feat == 12, 1.0, 0.0))
    for half in range(2):
        at = TILE * half
        qn = unit(dot(x, qkv_ref[:, at : at + TILE]))
        kn = unit(dot(x, qkv_ref[:, D + at : D + at + TILE]))
        vb = dot(x, qkv_ref[:, 2 * D + at : 2 * D + at + TILE]).astype(BF16)
        for sub in range(2):
            g = 2 * half + sub
            cut = slice(128 * sub, 128 * sub + 128)
            scale = jnp.ones((1, 128), F32)
            for h in range(GROUP):
                scale = jnp.where(own_head == h, scale_ref[g * GROUP + h], scale)
            whole = 100.0 / scale
            high = whole.astype(BF16).astype(F32)
            middle = (whole - high).astype(BF16).astype(F32)
            piece = jnp.where(feat < 4, high, jnp.where(feat < 8, middle, whole - high - middle))
            query_feat = jnp.where(
                feat < 12, jnp.where(region == feat % 4, piece, 0.0), jnp.where(feat == 12, -CENTRE, 0.0)
            )
            q_ref[g, :, 0:128] = qn[:, cut]
            q_ref[g, :, 128:256] = query_feat.astype(BF16)
            for h in range(GROUP):
                mine = own_head == h
                rows = slice(h * TOK, h * TOK + TOK)
                k_ref[g, rows, 0:128] = jnp.where(mine, kn[:, cut], jnp.zeros((), BF16))
                k_ref[g, rows, 128:256] = jnp.where(mine, key_feat, 0.0).astype(BF16)
                v_ref[g, rows, 0:128] = jnp.where(mine, vb[:, cut], jnp.zeros((), BF16))
                v_ref[g, rows, 128:256] = jnp.broadcast_to(jnp.where(mine, 1.0, 0.0), (TOK, 128)).astype(BF16)


def lane_scales(scale_ref, g):
    out = jnp.zeros((1, SPAN), F32)
    for h in range(GROUP):
        out = jnp.where(iota((1, SPAN), 1) // TOK == h, scale_ref[g * GROUP + h] * LOG2E, out)
    return out


def attend(q_ref, k_ref, v_ref, scale_ref, att_ref):
    least = jnp.full((TOK, 128), jnp.inf, F32)
    for g in range(HEADS // GROUP):
        scales = lane_scales(scale_ref, g)
        acc = None
        for j in range(SPAN // TILE):
            at = slice(TILE * j, TILE * j + TILE)
            powers = jnp.exp2(dot(q_ref[g], k_ref[g, at, :], NT) * scales[:, at]).astype(BF16)
            part = dot(powers, v_ref[g, at, :])
            acc = part if acc is None else acc + part
        total = acc[:, 128:]
        least = jnp.minimum(least, total)
        att_ref[:, 128 * g : 128 * g + 128] = (acc[:, :128] / total).astype(BF16)
    return jnp.min(least.reshape(TOK // 8, 8, 128), axis=0)


def attend_exact(q_ref, k_ref, v_ref, scale_ref, att_ref):
    def one(g, carry):
        scales = lane_scales(scale_ref, g)
        owner = iota((1, SPAN), 1) // TOK

        def block(b, carry):
            rows = pl.ds(pl.multiple_of(b * QUAD, QUAD), QUAD)
            score = dot(q_ref[g, rows, :], k_ref[g], NT) * scales
            top = jnp.zeros_like(score)
            for h in range(GROUP):
                peak = jnp.max(jnp.where(owner == h, score, -jnp.inf), axis=-1, keepdims=True)
                top = jnp.where(owner == h, peak, top)
            acc = dot(jnp.exp2(score - top).astype(BF16), v_ref[g])
            att_ref[g, rows, :] = (acc[:, :128] / acc[:, 128:]).astype(BF16)
            return carry

        return lax.fori_loop(0, TOK // QUAD, block, carry)

    lax.fori_loop(0, HEADS // GROUP, one, 0)


def attention_kernel(
    limits, tokens_ref, qkv_hbm, proj_hbm, gain_ref, scale_ref, x_ref, x1_ref, least_ref,
    send, recv, qkv_ref, proj_ref, q_ref, k_ref, v_ref, att_ref, load_sem, send_sem, recv_sem,
):
    tall, wide = lax.axis_index("tall"), lax.axis_index("wide")
    n_tall, n_wide = lax.axis_size("tall"), lax.axis_size("wide")
    loads = [
        pltpu.make_async_copy(qkv_hbm, qkv_ref, load_sem.at[0]),
        pltpu.make_async_copy(proj_hbm, proj_ref, load_sem.at[1]),
    ]
    for load in loads:
        load.start()
    up, left = lax.rem(tall + n_tall - 1, n_tall), lax.rem(wide + n_wide - 1, n_wide)
    down, right = lax.rem(tall + 1, n_tall), lax.rem(wide + 1, n_wide)
    targets = [(left_of, up_of) for left_of, up_of in ((wide, up), (left, tall), (left, up))]
    sources = [(wide, down), (right, tall), (right, down)]
    barrier = pltpu.get_barrier_semaphore()
    for peer in targets + sources:
        pl.semaphore_signal(barrier, inc=1, device_id=peer, device_id_type=MESH)
    place = iota((TOK, TOK), 0)
    quad, rest = place // QUAD, place % QUAD
    row = rest // HALF + jnp.where(quad % 2 == 0, HALF, 0)
    col = rest % HALF + jnp.where(quad < 2, HALF, 0)
    pick = (iota((TOK, TOK), 1) == row * EDGE + col).astype(BF16)
    send[...] = dot(pick, tokens_ref[...]).astype(BF16)
    recv[0:QUAD, :] = send[0:QUAD, :]
    pl.semaphore_wait(barrier, 6)
    copies = []
    for i, peer in enumerate(targets):
        rows = pl.ds(QUAD * (i + 1), QUAD)
        copies.append(
            pltpu.make_async_remote_copy(
                src_ref=send.at[rows], dst_ref=recv.at[rows], send_sem=send_sem.at[i], recv_sem=recv_sem.at[i],
                device_id=peer, device_id_type=MESH,
            )
        )
        copies[-1].start()
    row, col = place // EDGE, place % EDGE
    quad = (row // HALF) + 2 * (col // HALF)
    pick = (iota((TOK, TOK), 1) == quad * QUAD + (row % HALF) * HALF + col % HALF).astype(BF16)
    for load in loads:
        load.wait()
    for copy in copies:
        copy.wait()
    x = dot(pick, recv[...]).astype(BF16)
    x_ref[...] = x
    prepare(x, qkv_ref, scale_ref, region_column(*limits), q_ref, k_ref, v_ref)
    least_ref[...] = attend(q_ref, k_ref, v_ref, scale_ref, att_ref)
    out = dot(att_ref[...], proj_ref[...])
    x1_ref[...] = (x_ref[...].astype(F32) + norm(out, gain_ref[...])).astype(BF16)


def dispatch_kernel(
    limits, experts, x_hbm, x1_in, least_ref, ids_ref, keep_ref, qkv_hbm, proj_hbm, gain_ref, scale_ref,
    x1_ref, slots_ref, target_ref, x_ref, qkv_ref, proj_ref, q_ref, k_ref, v_ref, att_ref,
):
    x1_ref[...] = x1_in[...]

    @pl.when(jnp.logical_not(jnp.min(least_ref[...]) >= SAFE))
    def _():
        pltpu.sync_copy(x_hbm, x_ref)
        pltpu.sync_copy(qkv_hbm, qkv_ref)
        pltpu.sync_copy(proj_hbm, proj_ref)
        prepare(x_ref[...], qkv_ref, scale_ref, region_column(*limits), q_ref, k_ref, v_ref)
        attend_exact(q_ref, k_ref, v_ref, scale_ref, att_ref)
        out = dot(att_ref[0], proj_ref[0:128, :])
        for g in range(1, HEADS // GROUP):
            out += dot(att_ref[g], proj_ref[128 * g : 128 * g + 128, :])
        x1_ref[...] = (x_ref[...].astype(F32) + norm(out, gain_ref[...])).astype(BF16)

    ids, kept = ids_ref[...], keep_ref[...] == 1
    named = iota((experts, TOK), 0) == ids
    live = jnp.where(jnp.logical_and(named, kept), 1.0, 0.0).astype(BF16)
    earlier = (iota((TOK, TOK), 0) < iota((TOK, TOK), 1)).astype(BF16)
    slot = jnp.sum(jnp.where(named, dot(live, earlier), 0.0), axis=0, keepdims=True).astype(I32)
    target = jnp.where(kept, ids * ROOM + slot, -1)
    target_ref[...] = target
    spread = (iota((experts * ROOM, TOK), 0) == target).astype(BF16)
    slots_ref[...] = dot(spread, x1_ref[...]).astype(BF16)


def expert_kernel(
    experts, slots_ref, x1_ref, target_ref, router_ref, gain_ref, in_hbm, out_hbm, result_ref,
    arrived, made, back, acc, spread, gate, w_in, w_out, own_sem, give_sem, take_sem, ring_send, ring_recv,
):
    tall, wide = lax.axis_index("tall"), lax.axis_index("wide")
    n_tall, n_wide = lax.axis_size("tall"), lax.axis_size("wide")
    last = n_tall // 2
    down, up = lax.rem(tall + 1, n_tall), lax.rem(tall + n_tall - 1, n_tall)
    barrier = pltpu.get_barrier_semaphore()

    def partner(k):
        step = (k // 2) % 8
        size = (step + 1) // 2
        dy = size + (step + 1) % 2 * (8 - 2 * size)
        dx, dc = k // 16, k % 2
        core, x, y = wide % 2, (wide // 2) % 4, wide // 8
        return ((y + dy) % 8 * 4 + (x + dx) % 4) * 2 + (core + dc) % 2

    def greet(k, carry):
        pl.semaphore_signal(barrier, inc=1, device_id=(partner(k), tall), device_id_type=MESH)
        return carry

    for peer in (up, down):
        pl.semaphore_signal(barrier, inc=1, device_id=(wide, peer), device_id_type=MESH)
    lax.fori_loop(1, n_wide, greet, 0)
    own = [
        pltpu.make_async_copy(in_hbm, w_in.at[tall], own_sem.at[0]),
        pltpu.make_async_copy(out_hbm, w_out.at[tall], own_sem.at[1]),
        pltpu.make_async_copy(slots_ref.at[pl.ds(wide * ROOM, ROOM)], arrived.at[pl.ds(wide * ROOM, ROOM)], own_sem.at[2]),
    ]
    for copy in own:
        copy.start()
    pl.semaphore_wait(barrier, n_wide + 1)

    def hop(way, step, kind):
        owner = lax.rem(tall + n_tall + (1 - step if way == 0 else step - 1), n_tall)
        whole = (w_in, w_out)[kind].at[owner]
        return pltpu.make_async_remote_copy(
            src_ref=(in_hbm, out_hbm)[kind] if step == 1 else whole,
            dst_ref=whole,
            send_sem=ring_send.at[way, step - 1, kind],
            recv_sem=ring_recv.at[way, step - 1, kind],
            device_id=(wide, down if way == 0 else up),
            device_id_type=MESH,
        )

    def pieces(step):
        return [(0, 0), (1, 1)] if step == last else [(0, 0), (1, 0), (0, 1), (1, 1)]

    hops = {}
    def launch(step):
        for way, kind in pieces(step):
            hops[step, way, kind] = hop(way, step, kind)
            hops[step, way, kind].start()

    def arrive(step):
        for way, kind in pieces(step):
            hops[step, way, kind].wait_recv()

    def exchange(source, landing, phase):
        def one(k, carry):
            peer = partner(k)
            pltpu.make_async_remote_copy(
                src_ref=source.at[pl.ds(pl.multiple_of(peer * ROOM, ROOM), ROOM)],
                dst_ref=landing.at[pl.ds(pl.multiple_of(wide * ROOM, ROOM), ROOM)],
                send_sem=give_sem.at[phase],
                recv_sem=take_sem.at[phase],
                device_id=(peer, tall),
                device_id_type=MESH,
            ).start()
            return carry

        lax.fori_loop(1, n_wide, one, 0)

    def all_of(source, landing, phase):
        rows = pl.ds(0, (n_wide - 1) * ROOM)
        return pltpu.make_async_remote_copy(
            src_ref=source.at[rows], dst_ref=landing.at[rows], send_sem=give_sem.at[phase],
            recv_sem=take_sem.at[phase], device_id=(wide, down), device_id_type=MESH,
        )

    launch(1)
    exchange(slots_ref, arrived, 0)

    target = target_ref[...]
    spread[...] = (iota((experts * ROOM, TOK), 0) == target).astype(BF16)
    live = (iota((experts, TOK), 0) == target // ROOM).astype(BF16)
    eye = (iota((experts, experts), 0) == iota((experts, experts), 1)).astype(BF16)
    chosen = dot(live, eye, TN)
    logit = jnp.sum(dot(x1_ref[...], router_ref[...]) * chosen, axis=-1, keepdims=True)
    kept = jnp.sum(chosen, axis=-1, keepdims=True)
    gate[...] = jnp.broadcast_to(kept * jax.nn.sigmoid(logit), gate.shape)

    def chunk(owner, first=False):
        def rows(b, carry):
            at = pl.ds(pl.multiple_of(b * TILE, TILE), TILE)
            hidden = gelu(dot(arrived[at, :], w_in[owner])).astype(BF16)
            part = dot(hidden, w_out[owner])
            acc[at, :] = part if first else acc[at, :] + part
            return carry

        lax.fori_loop(0, experts * ROOM // TILE, rows, 0)

    arrive(1)
    launch(2)
    for copy in own:
        copy.wait()
    all_of(slots_ref, arrived, 0).wait_recv()
    chunk(tall, True)
    chunk(lax.rem(tall + n_tall - 1, n_tall))
    chunk(lax.rem(tall + 1, n_tall))
    for step in range(2, last + 1):
        arrive(step)
        if step < last:
            launch(step + 1)
            chunk(lax.rem(tall + n_tall - step, n_tall))
        chunk(lax.rem(tall + step, n_tall))
    made[...] = acc[...].astype(BF16)
    mine = pltpu.make_async_copy(
        made.at[pl.ds(wide * ROOM, ROOM)], back.at[pl.ds(wide * ROOM, ROOM)], own_sem.at[2]
    )
    mine.start()
    exchange(made, back, 1)
    mine.wait()
    all_of(slots_ref, arrived, 0).wait_send()
    for copy in hops.values():
        copy.wait_send()
    all_of(made, back, 1).wait_recv()
    picked = dot(spread[...], back[...], TN)
    result_ref[...] = (
        x1_ref[...].astype(F32) + gate[:, 0:1] * norm(picked, gain_ref[...])
    ).astype(BF16)
    all_of(made, back, 1).wait_send()


def body(
    tokens, qkv_weight, proj_weight, head_scale, attn_gain, router, expert_in, expert_out, moe_gain, expert_ids, keep
):
    n_tall, n_wide = lax.axis_size("tall"), lax.axis_size("wide")
    experts = router.shape[1]
    limits = (EDGE * n_tall, EDGE * n_wide)
    hidden = expert_in.shape[2]
    grid_shape = jax.ShapeDtypeStruct((TOK, D), BF16)
    qkv_scratch = [
        pltpu.VMEM((D, 3 * D), BF16),
        pltpu.VMEM((D, D), BF16),
        pltpu.VMEM((HEADS // GROUP, TOK, TILE), BF16),
        pltpu.VMEM((HEADS // GROUP, SPAN, TILE), BF16),
        pltpu.VMEM((HEADS // GROUP, SPAN, TILE), BF16),
    ]
    DMA = pltpu.SemaphoreType.DMA
    x, x1, least = pl.pallas_call(
        functools.partial(attention_kernel, limits),
        out_shape=(grid_shape, grid_shape, jax.ShapeDtypeStruct((8, 128), F32)),
        in_specs=[VMEM, ANY, ANY, VMEM, SMEM],
        out_specs=(VMEM, VMEM, VMEM),
        scratch_shapes=[pltpu.VMEM((TOK, D), BF16), pltpu.VMEM((TOK, D), BF16)]
        + qkv_scratch
        + [pltpu.VMEM((TOK, D), BF16), DMA((2,)), DMA((3,)), DMA((3,))],
        compiler_params=pltpu.CompilerParams(collective_id=0, has_side_effects=True, vmem_limit_bytes=50 << 20),
        name="attention",
    )(tokens.reshape(TOK, D), qkv_weight, proj_weight, attn_gain.reshape(1, D), head_scale)
    slot_shape = jax.ShapeDtypeStruct((experts * ROOM, D), BF16)
    x1, slots, target = pl.pallas_call(
        functools.partial(dispatch_kernel, limits, experts),
        out_shape=(grid_shape, slot_shape, jax.ShapeDtypeStruct((1, TOK), I32)),
        in_specs=[ANY, VMEM, VMEM, VMEM, VMEM, ANY, ANY, VMEM, SMEM],
        out_specs=(VMEM, VMEM, VMEM),
        scratch_shapes=[pltpu.VMEM((TOK, D), BF16)]
        + qkv_scratch
        + [pltpu.VMEM((HEADS // GROUP, TOK, 128), BF16)],
        compiler_params=pltpu.CompilerParams(vmem_limit_bytes=50 << 20),
        name="dispatch",
    )(
        x, x1, least, expert_ids.reshape(1, TOK), keep.reshape(1, TOK), qkv_weight, proj_weight,
        attn_gain.reshape(1, D), head_scale,
    )
    slot_buffer = pltpu.VMEM((experts * ROOM, D), BF16)
    out = pl.pallas_call(
        functools.partial(expert_kernel, experts),
        out_shape=grid_shape,
        in_specs=[VMEM, VMEM, VMEM, VMEM, VMEM, ANY, ANY],
        out_specs=VMEM,
        scratch_shapes=[
            slot_buffer,
            slot_buffer,
            slot_buffer,
            pltpu.VMEM((experts * ROOM, D), F32),
            pltpu.VMEM((experts * ROOM, TOK), BF16),
            pltpu.VMEM((TOK, 128), F32),
            pltpu.VMEM((n_tall, D, hidden), BF16),
            pltpu.VMEM((n_tall, hidden, D), BF16),
            DMA((3,)),
            DMA((2,)),
            DMA((2,)),
            DMA((2, n_tall // 2, 2)),
            DMA((2, n_tall // 2, 2)),
        ],
        compiler_params=pltpu.CompilerParams(collective_id=1, has_side_effects=True, vmem_limit_bytes=50 << 20),
        name="experts",
    )(slots, x1, target, router, moe_gain.reshape(1, D), expert_in[0], expert_out[0])
    return out.reshape(EDGE, EDGE, D)


def solution(mesh):
    placed = (
        P("tall", "wide", None), P(), P(), P(), P(), P(), P("wide", None, "tall"), P("wide", "tall", None), P(),
        P("tall", "wide", None, None), P("tall", "wide", None),
    )
    return jax.shard_map(
        body, mesh=mesh, in_specs=placed, out_specs=P("tall", "wide", None), check_vma=False
    )
```

time: 209 us -> 131 us (0.63)
  Pallas kernels: 0 us -> 125 us
  matrix products: 61.2 us -> 0 us
  blocking collectives: 38.6 us -> 0 us
  waiting for transfers between devices: 36 us -> 0 us
  starting transfers between devices: 21.4 us -> 0 us
  local copies, waits for them, and re-layouts: 25.2 us -> 5.83 us
  between operations: 13.7 us -> 0.12 us
  other arithmetic: 11.5 us -> 0 us
    pallas_call x0 -> x3, Pallas kernels: none -> 125 us  [the longest x1 96.1 us: body(): pl.pallas_call(functools.partial(expert_kernel, experts), out_shape=grid_...]
    dot_general x8 -> x0, matrix products: 39.1 us -> none  [the longest x1 19.6 us: body(): produced = jnp.dot(hidden, full_out, preferred_element_type=jnp.float32)]
    all_to_all x1 -> x0, blocking collectives: 38.6 us -> none  [body(): lax.all_to_all(outgoing, 'wide', split_axis=0, concat_axis=0, tiled=True)]
    all_to_all x1 -> x0, waiting for transfers between devices: 27.6 us -> none  [body(): lax.all_to_all(produced.astype(jnp.bfloat16).reshape(experts, capacity, f...]
    sub x4 -> x0, matrix products: 22.1 us -> none  [one_group(): weights_soft = jax.nn.softmax(scores, axis=-1).astype(jnp.bfloat16)]
    ppermute x2 -> x0, starting transfers between devices: 15 us -> none  [shifted(): lax.ppermute(value, axis, [(i, (i + by) % peers) for i in range(peers)])]
    ppermute x2 -> x0, waiting for transfers between devices: 7.65 us -> none  [shifted(): lax.ppermute(value, axis, [(i, (i + by) % peers) for i in range(peers)])]
    slice x7 -> x0, local copies, waits for them, and re-layouts: 7.26 us -> none  [the longest x2 3.3 us: window_attention(): key_heads = unit_heads(project[:, feature:2 * feature], head_count)]
  transfers between devices with their start and end apart: 5 -> 0, of which waited for: 3 -> 0; matrix products, arithmetic and copies ran while one was open for 32% -> 0% of each run, Pallas kernels for 0% -> 0%
where the time goes in v1:
time: 131 us
  Pallas kernels  125 us (95%)
  local copies, waits for them, and re-layouts  5.83 us (4%)
    pallas_call x1, Pallas kernels, body(): pl.pallas_call(functools.partial(expert_kernel, experts), out_shape=grid_...  96.1 us
    pallas_call x1, Pallas kernels, body(): pl.pallas_call(functools.partial(attention_kernel, limits), out_shape=(gr...  26.6 us
    unnamed x26, local copies, waits for them, and re-layouts  5.83 us

profile of v1, /device:TPU:1, one launch (start us, length us, event | category | flops | bytes accessed | tf_op | source)
XLA Modules:
  0.0 130.7 jit_solution(8497392925417363628)
XLA Ops:
  0.0 0.0 copy-start.7
  0.0 0.0 copy-start
  0.0 1.4 %copy-done = bf16[512,1536]{1,0:T(8,128)(2,1)S(1)} copy-done((bf16[512,1536]{1,0:T(8,128)(2,1)S(1)}, bf16[512,1536]{1,0:T(8,128)(2,1)}, u32[]{:S(2)}) %copy-start) | copy-done | bytes 1572888
  1.4 0.0 copy-start.1
  1.4 1.0 copy-done.1
  2.5 0.0 copy-start.3
  2.5 1.1 copy-done.3
  3.5 0.0 copy-start.6
  3.5 0.7 copy-done.6
  4.2 0.0 copy-start.10
  4.2 0.7 copy-done.10
  4.9 0.0 copy-start.2
  4.9 0.0 copy-start.8
  4.9 26.6 %attention.1 = (bf16[576,512]{1,0:T(8,128)(2,1)S(1)}, bf16[576,512]{1,0:T(8,128)(2,1)S(1)}, f32[8,128]{1,0:T(8,128)S(1)}) custom-call(bf16[576,512]{1,0:T(8,128)(2,1)S(1)} %bitcast.9, bf16[512,1536]{1,0:T(8,128)(2,1)S(1)} %copy-done, bf16[512,512]{1,0:T(8,128)(2,1)S(1)} %copy-done.1, f32[1,512]{1,0:T(1,128)S(1)} %bitcast.12, f32[16]{0:T(128)S(1)} %copy-done.10), custom_call_target="tpu_custom_call" | custom-call | tf_op jit(solution)/shard_map/attention/pallas_call | solution.py:384
  31.5 0.0 copy-done.7
  31.5 0.0 copy-done.2
  31.5 0.0 copy-done.8
  31.5 0.0 copy-start.11
  31.5 0.0 copy-start.4
  31.5 0.0 copy-start.5
  31.5 0.0 copy-start.9
  31.5 2.1 %dispatch.1 = (bf16[576,512]{1,0:T(8,128)(2,1)S(1)}, bf16[1024,512]{1,0:T(8,128)(2,1)S(1)}, s32[1,576]{1,0:T(1,128)S(1)}) custom-call(bf16[576,512]{1,0:T(8,128)(2,1)S(1)} %get-tuple-element.11.x_hbm, bf16[576,512]{1,0:T(8,128)(2,1)S(1)} %get-tuple-element.12.x1_in, f32[8,128]{1,0:T(8,128)S(1)} %get-tuple-element.13.least_ref, s32[1,576]{1,0:T(1,128)S(1)} %bitcast.14, ...), custom_call_target="tpu_custom_call" | custom-call | tf_op jit(solution)/shard_map/dispatch/pallas_call | solution.py:396
  33.6 0.0 copy-done.11
  33.6 0.1 copy.12.router_ref
  33.8 0.0 copy-done.4
  33.8 0.0 copy-done.5
  33.8 0.0 copy-done.9
  33.8 96.1 %experts.1 = bf16[576,512]{1,0:T(8,128)(2,1)S(1)} custom-call(bf16[1024,512]{1,0:T(8,128)(2,1)S(1)} %get-tuple-element.14.slots_ref, bf16[576,512]{1,0:T(8,128)(2,1)S(1)} %get-tuple-element.15.x1_ref, s32[1,576]{1,0:T(1,128)S(1)} %get-tuple-element.16.target_ref, bf16[512,64]{1,0:T(8,128)(2,1)S(1)} %copy.12.router_ref, f32[1,512]{1,0:T(1,128)S(1)} %bitcast.16, ...), custom_call_target="tpu_custom_call" | custom-call | tf_op jit(solution)/shard_map/experts/pallas_call | solution.py:411
  129.9 0.8 copy.14
Async XLA Ops:
  0.0 31.5 %copy-start.7 = (s32[1,1,576,1]{2,3,1,0:T(1,128)S(1)}, s32[1,1,576,1]{2,3,1,0:T(1,128)}, u32[]{:S(2)}) copy-start(s32[1,1,576,1]{2,3,1,0:T(1,128)} %param.20) | copy-start | bytes 6916
  0.0 1.4 %copy-start = (bf16[512,1536]{1,0:T(8,128)(2,1)S(1)}, bf16[512,1536]{1,0:T(8,128)(2,1)}, u32[]{:S(2)}) copy-start(bf16[512,1536]{1,0:T(8,128)(2,1)} %qkv_hbm.3) | copy-start | bytes 4718596
  1.4 1.0 copy-start.1
  2.5 1.1 copy-start.3
  3.5 0.7 copy-start.6
  4.2 0.7 copy-start.10
  4.9 26.6 %copy-start.2 = (bf16[512,512]{1,0:T(8,128)(2,1)S(1)}, bf16[512,512]{1,0:T(8,128)(2,1)}, u32[]{:S(2)}) copy-start(bf16[512,512]{1,0:T(8,128)(2,1)} %proj_hbm.3) | copy-start | bytes 1572868
  4.9 26.6 %copy-start.8 = (s32[1,1,576]{2,1,0:T(1,128)S(1)}, s32[1,1,576]{2,1,0:T(1,128)}, u32[]{:S(2)}) copy-start(s32[1,1,576]{2,1,0:T(1,128)} %param.21) | copy-start | bytes 6916
  31.5 2.1 %copy-start.11 = (bf16[512,64]{0,1:T(8,128)(2,1)S(1)}, bf16[512,64]{0,1:T(8,128)(2,1)}, u32[]{:S(2)}) copy-start(bf16[512,64]{0,1:T(8,128)(2,1)} %param.16) | copy-start | bytes 196612
  31.5 2.3 %copy-start.4 = (bf16[1,512,256]{2,1,0:T(8,128)(2,1)S(1)}, bf16[1,512,256]{2,1,0:T(8,128)(2,1)}, u32[]{:S(2)}) copy-start(bf16[1,512,256]{2,1,0:T(8,128)(2,1)} %param.17) | copy-start | bytes 786436
  31.5 2.3 %copy-start.5 = (bf16[1,256,512]{2,1,0:T(8,128)(2,1)S(1)}, bf16[1,256,512]{2,1,0:T(8,128)(2,1)}, u32[]{:S(2)}) copy-start(bf16[1,256,512]{2,1,0:T(8,128)(2,1)} %param.18) | copy-start | bytes 786436
  31.5 2.3 %copy-start.9 = (f32[512]{0:T(512)S(1)}, f32[512]{0:T(512)}, u32[]{:S(2)}) copy-start(f32[512]{0:T(512)} %param.19) | copy-start | bytes 6148

commit v2 on v1

v2 whole, which is shorter than its diff:
```python
import functools
import math

import jax
import jax.numpy as jnp
from jax import lax
from jax.experimental import pallas as pl
from jax.experimental.pallas import tpu as pltpu
from jax.sharding import PartitionSpec as P

F32, BF16, I32 = jnp.float32, jnp.bfloat16, jnp.int32
MESH = pl.DeviceIdType.MESH
EDGE = 24
HALF = EDGE // 2
TOK = EDGE * EDGE
QUAD = HALF * HALF
HEADS = 16
HEAD = 32
D = 512
GROUP = 4
SPAN = GROUP * TOK
TILE = 256
LOG2E = math.log2(math.e)
CENTRE = 0.375
SAFE = 2.0**-60
ROOM = 13
LANES = 128
WAYS = D // LANES
NT = (((1,), (1,)), ((), ()))
TN = (((0,), (0,)), ((), ()))
VMEM = pl.BlockSpec(memory_space=pltpu.VMEM)
SMEM = pl.BlockSpec(memory_space=pltpu.SMEM)
HBM = pl.BlockSpec(memory_space=pltpu.HBM)


def dot(a, b, dims=None):
    if dims is None:
        return jnp.dot(a, b, preferred_element_type=F32)
    return lax.dot_general(a, b, dims, preferred_element_type=F32)


def iota(shape, axis):
    return lax.broadcasted_iota(I32, shape, axis)


def norm(value, gain):
    mean = jnp.mean(value, axis=-1, keepdims=True)
    centred = value - mean
    return centred * lax.rsqrt(jnp.mean(centred * centred, axis=-1, keepdims=True) + 1e-5) * gain


def gelu(value):
    return 0.5 * value * (1.0 + lax.erf(value * math.sqrt(0.5)))


def unit(block):
    ones = (iota((TILE, TILE), 0) // HEAD == iota((TILE, TILE), 1) // HEAD).astype(BF16)
    square = block * block
    high = square.astype(BF16)
    low = (square - high.astype(F32)).astype(BF16)
    return (block * lax.rsqrt(dot(high, ones) + dot(low, ones) + 1e-6)).astype(BF16)


def region_column(total_rows, total_cols):
    place = iota((TOK, 1), 0)
    row = lax.axis_index("tall") * EDGE + place // EDGE
    col = lax.axis_index("wide") * EDGE + place % EDGE
    return (row + HALF >= total_rows).astype(I32) * 2 + (col + HALF >= total_cols).astype(I32)


def features(scale_ref, region, q_ref, k_ref, v_ref):
    lane = iota((1, 128), 1)
    feat, own_head = lane % HEAD, lane // HEAD
    key_feat = jnp.where(feat < 12, jnp.where(region == feat % 4, 0.0, -1.0), jnp.where(feat == 12, 1.0, 0.0))
    for g in range(HEADS // GROUP):
        scale = jnp.ones((1, 128), F32)
        for h in range(GROUP):
            scale = jnp.where(own_head == h, scale_ref[g * GROUP + h], scale)
        whole = 100.0 / scale
        high = whole.astype(BF16).astype(F32)
        middle = (whole - high).astype(BF16).astype(F32)
        piece = jnp.where(feat < 4, high, jnp.where(feat < 8, middle, whole - high - middle))
        query_feat = jnp.where(
            feat < 12, jnp.where(region == feat % 4, piece, 0.0), jnp.where(feat == 12, -CENTRE, 0.0)
        )
        q_ref[g, :, 128:256] = query_feat.astype(BF16)
        for h in range(GROUP):
            mine = own_head == h
            rows = slice(h * TOK, h * TOK + TOK)
            k_ref[g, rows, 128:256] = jnp.where(mine, key_feat, 0.0).astype(BF16)
            v_ref[g, rows, 128:256] = jnp.broadcast_to(jnp.where(mine, 1.0, 0.0), (TOK, 128)).astype(BF16)


def prepare(x, qkv_ref, q_ref, k_ref, v_ref):
    own_head = iota((1, 128), 1) // HEAD
    for half in range(2):
        at = TILE * half
        qn = unit(dot(x, qkv_ref[:, at : at + TILE]))
        kn = unit(dot(x, qkv_ref[:, D + at : D + at + TILE]))
        vb = dot(x, qkv_ref[:, 2 * D + at : 2 * D + at + TILE]).astype(BF16)
        for sub in range(2):
            g = 2 * half + sub
            cut = slice(128 * sub, 128 * sub + 128)
            q_ref[g, :, 0:128] = qn[:, cut]
            for h in range(GROUP):
                mine = own_head == h
                rows = slice(h * TOK, h * TOK + TOK)
                k_ref[g, rows, 0:128] = jnp.where(mine, kn[:, cut], jnp.zeros((), BF16))
                v_ref[g, rows, 0:128] = jnp.where(mine, vb[:, cut], jnp.zeros((), BF16))


def lane_scales(scale_ref, g):
    out = jnp.zeros((1, SPAN), F32)
    for h in range(GROUP):
        out = jnp.where(iota((1, SPAN), 1) // TOK == h, scale_ref[g * GROUP + h] * LOG2E, out)
    return out


def attend(q_ref, k_ref, v_ref, scale_ref, att_ref, between):
    least = jnp.full((TOK, 128), jnp.inf, F32)
    for g in range(HEADS // GROUP):
        scales = lane_scales(scale_ref, g)
        acc = None
        for j in range(SPAN // TILE):
            at = slice(TILE * j, TILE * j + TILE)
            powers = jnp.exp2(dot(q_ref[g], k_ref[g, at, :], NT) * scales[:, at]).astype(BF16)
            part = dot(powers, v_ref[g, at, :])
            acc = part if acc is None else acc + part
        total = acc[:, 128:]
        least = jnp.minimum(least, total)
        att_ref[:, 128 * g : 128 * g + 128] = (acc[:, :128] / total).astype(BF16)
        between(g)
    return jnp.min(least.reshape(TOK // 8, 8, 128), axis=0)


def attend_exact(q_ref, k_ref, v_ref, scale_ref, att_ref):
    def one(g, carry):
        scales = lane_scales(scale_ref, g)
        owner = iota((1, SPAN), 1) // TOK

        def block(b, carry):
            rows = pl.ds(pl.multiple_of(b * QUAD, QUAD), QUAD)
            score = dot(q_ref[g, rows, :], k_ref[g], NT) * scales
            top = jnp.zeros_like(score)
            for h in range(GROUP):
                peak = jnp.max(jnp.where(owner == h, score, -jnp.inf), axis=-1, keepdims=True)
                top = jnp.where(owner == h, peak, top)
            acc = dot(jnp.exp2(score - top).astype(BF16), v_ref[g])
            att_ref[g, rows, :] = (acc[:, :128] / acc[:, 128:]).astype(BF16)
            return carry

        return lax.fori_loop(0, TOK // QUAD, block, carry)

    lax.fori_loop(0, HEADS // GROUP, one, 0)


def ring_hop(own, gathered, way, step, send_sem, recv_sem):
    tall, wide, n_tall = lax.axis_index("tall"), lax.axis_index("wide"), lax.axis_size("tall")
    owner = lax.rem(tall + n_tall + (1 - step if way == 0 else step - 1), n_tall)
    return pltpu.make_async_remote_copy(
        src_ref=own if step == 1 else gathered.at[owner],
        dst_ref=gathered.at[owner],
        send_sem=send_sem.at[way, step - 1],
        recv_sem=recv_sem.at[way, step - 1],
        device_id=(wide, lax.rem(tall + (1 if way == 0 else n_tall - 1), n_tall)),
        device_id_type=MESH,
    )


def attention_kernel(
    limits, tokens_hbm, qkv_hbm, proj_hbm, gain_ref, scale_ref, in_hbm, x_ref, x1_ref, least_ref, w_in,
    tokens_ref, send, recv, qkv_ref, proj_ref, q_ref, k_ref, v_ref, att_ref, load_sem, send_sem, recv_sem,
    ring_send, ring_recv,
):
    tall, wide = lax.axis_index("tall"), lax.axis_index("wide")
    n_tall, n_wide = lax.axis_size("tall"), lax.axis_size("wide")
    loads = [
        pltpu.make_async_copy(tokens_hbm, tokens_ref, load_sem.at[0]),
        pltpu.make_async_copy(qkv_hbm, qkv_ref, load_sem.at[1]),
        pltpu.make_async_copy(proj_hbm, proj_ref, load_sem.at[2]),
        pltpu.make_async_copy(in_hbm, w_in.at[tall], load_sem.at[3]),
    ]
    for load in loads:
        load.start()
    up, left = lax.rem(tall + n_tall - 1, n_tall), lax.rem(wide + n_wide - 1, n_wide)
    down, right = lax.rem(tall + 1, n_tall), lax.rem(wide + 1, n_wide)
    targets = [(wide, up), (left, tall), (left, up)]
    sources = [(wide, down), (right, tall), (right, down)]
    barrier = pltpu.get_barrier_semaphore()
    for peer in targets + sources:
        pl.semaphore_signal(barrier, inc=1, device_id=peer, device_id_type=MESH)
    place = iota((TOK, TOK), 0)
    quad, rest = place // QUAD, place % QUAD
    row = rest // HALF + jnp.where(quad % 2 == 0, HALF, 0)
    col = rest % HALF + jnp.where(quad < 2, HALF, 0)
    pick = (iota((TOK, TOK), 1) == row * EDGE + col).astype(BF16)
    loads[0].wait()
    send[...] = dot(pick, tokens_ref[...]).astype(BF16)
    pl.semaphore_wait(barrier, 6)
    copies = []
    for i, peer in enumerate(targets):
        rows = pl.ds(QUAD * (i + 1), QUAD)
        copies.append(
            pltpu.make_async_remote_copy(
                src_ref=send.at[rows], dst_ref=recv.at[rows], send_sem=send_sem.at[i], recv_sem=recv_sem.at[i],
                device_id=peer, device_id_type=MESH,
            )
        )
        copies[-1].start()
    hops = {}

    def launch(way, step):
        hops[way, step] = ring_hop(in_hbm, w_in, way, step, ring_send, ring_recv)
        hops[way, step].start()

    def onward(way, step):
        hops[way, step].wait_recv()
        launch(way, step + 1)

    launch(0, 1)
    recv[0:QUAD, :] = send[0:QUAD, :]
    row, col = place // EDGE, place % EDGE
    quad = (row // HALF) + 2 * (col // HALF)
    pick = (iota((TOK, TOK), 1) == quad * QUAD + (row % HALF) * HALF + col % HALF).astype(BF16)
    features(scale_ref, region_column(*limits), q_ref, k_ref, v_ref)
    for load in loads[1:]:
        load.wait()
    for copy in copies:
        copy.wait()
    launch(1, 1)
    onward(0, 1)
    x = dot(pick, recv[...]).astype(BF16)
    x_ref[...] = x
    prepare(x, qkv_ref, q_ref, k_ref, v_ref)

    def between(g):
        if g == 1:
            onward(1, 1)
            onward(0, 2)

    least_ref[...] = attend(q_ref, k_ref, v_ref, scale_ref, att_ref, between)
    out = dot(att_ref[...], proj_ref[...])
    x1_ref[...] = (x_ref[...].astype(F32) + norm(out, gain_ref[...])).astype(BF16)
    hops[1, 2].wait_recv()
    hops[0, 3].wait_recv()
    for hop in hops.values():
        hop.wait_send()


def rem(a, n):
    return lax.rem(a, jnp.int32(n))


def div(a, n):
    return lax.div(a, jnp.int32(n))


def partner(k, sign):
    wide = lax.axis_index("wide")
    core, x, y = rem(wide, 2), rem(div(wide, 2), 4), div(wide, 8)
    turn = rem(64 - k, 64)
    step = rem(turn, 8)
    size = div(step + 1, 2)
    dy = size + rem(step + 1, 2) * (8 - 2 * size)
    dx, dc = rem(div(turn, 8), 4), div(turn, 32)
    return (rem(y + 8 + sign * dy, 8) * 4 + rem(x + 4 + sign * dx, 4)) * 2 + rem(core + 2 + sign * dc, 2)


def place_of(expert):
    wide = lax.axis_index("wide")
    dc = (expert % 2 + 2 - wide % 2) % 2
    dx = (expert // 2 % 4 + 4 - wide // 2 % 4) % 4
    dy = (expert // 8 + 8 - wide // 8) % 8
    step = jnp.where(dy == 0, 0, jnp.where(dy <= 4, 2 * dy - 1, 16 - 2 * dy))
    return (64 - (dc * 32 + dx * 8 + step)) % 64


def dispatch_kernel(
    limits, experts, x_hbm, x1_in, least_ref, ids_ref, keep_ref, qkv_hbm, proj_hbm, gain_ref, scale_ref,
    x1_ref, slots_ref, target_ref, x_ref, qkv_ref, proj_ref, q_ref, k_ref, v_ref, att_ref,
):
    x1_ref[...] = x1_in[...]

    @pl.when(jnp.logical_not(jnp.min(least_ref[...]) >= SAFE))
    def _():
        pltpu.sync_copy(x_hbm, x_ref)
        pltpu.sync_copy(qkv_hbm, qkv_ref)
        pltpu.sync_copy(proj_hbm, proj_ref)
        features(scale_ref, region_column(*limits), q_ref, k_ref, v_ref)
        prepare(x_ref[...], qkv_ref, q_ref, k_ref, v_ref)
        attend_exact(q_ref, k_ref, v_ref, scale_ref, att_ref)
        out = dot(att_ref[0], proj_ref[0:128, :])
        for g in range(1, HEADS // GROUP):
            out += dot(att_ref[g], proj_ref[128 * g : 128 * g + 128, :])
        x1_ref[...] = (x_ref[...].astype(F32) + norm(out, gain_ref[...])).astype(BF16)

    ids, kept = ids_ref[...], keep_ref[...] == 1
    named = iota((experts, TOK), 0) == ids
    live = jnp.where(jnp.logical_and(named, kept), 1.0, 0.0).astype(BF16)
    earlier = (iota((TOK, TOK), 0) < iota((TOK, TOK), 1)).astype(BF16)
    slot = jnp.sum(jnp.where(named, dot(live, earlier), 0.0), axis=0, keepdims=True).astype(I32)
    target = jnp.where(kept, place_of(ids) * ROOM + slot, -1)
    target_ref[...] = target
    spread = (iota((experts * ROOM, TOK), 0) == target).astype(BF16)
    slots_ref[...] = dot(spread, x1_ref[...]).astype(BF16).reshape(experts * ROOM, WAYS, LANES)


def expert_kernel(
    experts, slots_ref, x1_ref, target_ref, ids_ref, router_ref, gain_ref, w_in_hbm, out_hbm, result_ref,
    arrived, made, back, hidden, picked, spread, gate, w_in, w_out, own_sem, give_send, give_recv, take_send, take_recv,
    in_send, in_recv, out_send, out_recv,
):
    tall, wide = lax.axis_index("tall"), lax.axis_index("wide")
    n_tall, n_wide = lax.axis_size("tall"), lax.axis_size("wide")
    last = n_tall // 2
    down, up = lax.rem(tall + 1, n_tall), lax.rem(tall + n_tall - 1, n_tall)
    barrier = pltpu.get_barrier_semaphore()

    def greet(k, carry):
        pl.semaphore_signal(barrier, inc=1, device_id=(rem(wide + k, n_wide), tall), device_id_type=MESH)
        return carry

    for peer in (up, down):
        pl.semaphore_signal(barrier, inc=1, device_id=(wide, peer), device_id_type=MESH)
    lax.fori_loop(1, n_wide, greet, 0)
    own = [pltpu.make_async_copy(out_hbm, w_out.at[tall], own_sem.at[0])]
    own.append(pltpu.make_async_copy(slots_ref.at[pl.ds(0, ROOM)], arrived.at[pl.ds(0, ROOM)], own_sem.at[1]))
    for i in range(1 - last, last - 1):
        block = lax.rem(tall + n_tall + i, n_tall)
        own.append(pltpu.make_async_copy(w_in_hbm.at[block], w_in.at[block], own_sem.at[2 + last + i]))
    for copy in own:
        copy.start()
    pl.semaphore_wait(barrier, n_wide + 1)

    hops, sent = {}, []

    def launch(step):
        for way in range(2):
            hops[step, way] = ring_hop(out_hbm, w_out, way, step, out_send, out_recv)
            hops[step, way].start()
            sent.append(hops[step, way])

    def arrive(step):
        for way in range(2):
            hops[step, way].wait_recv()

    def halfway():
        copies = []
        for way in range(2):
            owner = lax.rem(tall + (n_tall + 1 - last if way == 0 else last - 1), n_tall)
            rows = pl.ds(TILE // 2 * way, TILE // 2)
            copies.append(
                pltpu.make_async_remote_copy(
                    src_ref=w_out.at[owner, rows], dst_ref=w_out.at[owner, rows], send_sem=out_send.at[way, last - 1],
                    recv_sem=out_recv.at[way, last - 1], device_id=(wide, down if way == 0 else up),
                    device_id_type=MESH,
                )
            )
            copies[-1].start()
        sent.extend(copies)
        return copies

    def remainder(way):
        owner = lax.rem(tall + (n_tall + 1 - last if way == 0 else last - 2), n_tall)
        copy = pltpu.make_async_remote_copy(
            src_ref=w_in_hbm.at[owner], dst_ref=w_in.at[owner], send_sem=in_send.at[way], recv_sem=in_recv.at[way],
            device_id=(wide, down if way == 0 else up), device_id_type=MESH,
        )
        copy.start()
        sent.append(copy)
        return copy

    def exchange(source, landing, send_sem, recv_sem, sign, start, stop, group):
        def one(k, carry):
            rows = pl.ds(k * ROOM, ROOM)
            pltpu.make_async_remote_copy(
                src_ref=source.at[rows], dst_ref=landing.at[rows], send_sem=send_sem, recv_sem=recv_sem.at[group],
                device_id=(partner(k, sign), tall), device_id_type=MESH,
            ).start()
            return carry

        lax.fori_loop(start, stop, one, 0)

    def whole_of(ref, blocks, send_sem, recv_sem):
        rows = pl.ds(0, blocks * ROOM)
        return pltpu.make_async_remote_copy(
            src_ref=ref.at[rows], dst_ref=ref.at[rows], send_sem=send_sem, recv_sem=recv_sem,
            device_id=(wide, down), device_id_type=MESH,
        )

    per = 8
    groups = n_wide // per
    in_rest = [remainder(0), remainder(1)]
    launch(1)
    for group in range(groups):
        exchange(slots_ref, arrived, give_send.at[0], give_recv, 1, max(1, group * per), group * per + per, group)

    target = target_ref[...]
    live = jnp.where(jnp.logical_and(iota((experts, TOK), 0) == ids_ref[...], target >= 0), 1.0, 0.0)
    eye = (iota((experts, experts), 0) == iota((experts, experts), 1)).astype(BF16)
    chosen = dot(live.astype(BF16), eye, TN)
    slot = (jnp.maximum(target, 0) % ROOM).astype(F32)
    slot = jnp.sum(dot((live * slot).astype(BF16), eye, TN), axis=-1, keepdims=True)
    block = jnp.sum(chosen * place_of(iota((1, experts), 1)).astype(F32), axis=-1, keepdims=True)
    kept = jnp.sum(chosen, axis=-1, keepdims=True)
    landing = jnp.where(kept > 0.5, block * ROOM + slot, -1.0).astype(I32)
    span = 2 * per * ROOM
    for pair in range(groups // 2):
        spread[pair] = (iota((TOK, span), 1) + pair * span == landing).astype(BF16)
    logit = jnp.sum(dot(x1_ref[...], router_ref[...], NT) * chosen, axis=-1, keepdims=True)
    gate[...] = jnp.broadcast_to(kept * jax.nn.sigmoid(logit), gate.shape)

    def first(group):
        rows = slice(group * per * ROOM, (group + 1) * per * ROOM)
        whole_of(arrived, per - (group == 0), give_send.at[0], give_recv.at[group]).wait_recv()
        here = arrived[rows].reshape(per * ROOM, D)
        for c in range(n_tall):
            hidden[group, :, c * TILE : c * TILE + TILE] = gelu(dot(here, w_in[c])).astype(BF16)

    def second(group):
        rows = slice(group * per * ROOM, (group + 1) * per * ROOM)
        out = dot(hidden[group], w_out[...].reshape(n_tall * TILE, D)).astype(BF16)
        made[rows] = out.reshape(per * ROOM, WAYS, LANES)
        exchange(made, back, take_send.at[0], take_recv, -1, max(1, group * per), group * per + per, group)

    for copy in own:
        copy.wait()
    for copy in in_rest:
        copy.wait_recv()
    arrive(1)
    launch(2)
    for group in range(0, 2):
        first(group)
    arrive(2)
    launch(3)
    for group in range(2, 5):
        first(group)
    arrive(3)
    out_far = halfway()
    for group in range(5, groups):
        first(group)
    for copy in out_far:
        copy.wait_recv()
    for group in range(groups):
        second(group)
    mine = pltpu.make_async_copy(made.at[pl.ds(0, ROOM)], back.at[pl.ds(0, ROOM)], own_sem.at[1])
    mine.start()
    for copy in sent:
        copy.wait_send()
    whole_of(slots_ref, n_wide - 1, give_send.at[0], give_recv.at[0]).wait_send()
    mine.wait()
    for pair in range(groups // 2):
        for group in (2 * pair, 2 * pair + 1):
            whole_of(back, per - (group == 0), take_send.at[0], take_recv.at[group]).wait_recv()
        part = dot(spread[pair], back[pair * span : pair * span + span].reshape(span, D))
        if pair < groups // 2 - 1:
            picked[...] = part if pair == 0 else picked[...] + part
    result_ref[...] = (
        x1_ref[...].astype(F32) + gate[:, 0:1] * norm(picked[...] + part, gain_ref[...])
    ).astype(BF16)
    whole_of(made, n_wide - 1, take_send.at[0], take_recv.at[0]).wait_send()


def body(
    tokens, qkv_weight, proj_weight, head_scale, attn_gain, router, expert_in, expert_out, moe_gain, expert_ids, keep
):
    n_tall, n_wide = lax.axis_size("tall"), lax.axis_size("wide")
    experts = router.shape[1]
    limits = (EDGE * n_tall, EDGE * n_wide)
    hidden = expert_in.shape[2]
    grid_shape = jax.ShapeDtypeStruct((TOK, D), BF16)
    qkv_scratch = [
        pltpu.VMEM((D, 3 * D), BF16),
        pltpu.VMEM((D, D), BF16),
        pltpu.VMEM((HEADS // GROUP, TOK, TILE), BF16),
        pltpu.VMEM((HEADS // GROUP, SPAN, TILE), BF16),
        pltpu.VMEM((HEADS // GROUP, SPAN, TILE), BF16),
    ]
    DMA = pltpu.SemaphoreType.DMA
    x, x1, least, w_in = pl.pallas_call(
        functools.partial(attention_kernel, limits),
        out_shape=(
            grid_shape, grid_shape, jax.ShapeDtypeStruct((8, 128), F32), jax.ShapeDtypeStruct((n_tall, D, hidden), BF16)
        ),
        in_specs=[HBM, HBM, HBM, VMEM, SMEM, HBM],
        out_specs=(VMEM, VMEM, VMEM, HBM),
        scratch_shapes=[pltpu.VMEM((TOK, D), BF16)] * 3
        + qkv_scratch
        + [pltpu.VMEM((TOK, D), BF16), DMA((4,)), DMA((3,)), DMA((3,)), DMA((2, 3)), DMA((2, 3))],
        compiler_params=pltpu.CompilerParams(collective_id=0, has_side_effects=True, vmem_limit_bytes=62 << 20),
        name="attention",
    )(tokens.reshape(TOK, D), qkv_weight, proj_weight, attn_gain.reshape(1, D), head_scale, expert_in[0])
    slot_shape = jax.ShapeDtypeStruct((experts * ROOM, WAYS, LANES), BF16)
    ids = expert_ids.reshape(1, TOK)
    x1, slots, target = pl.pallas_call(
        functools.partial(dispatch_kernel, limits, experts),
        out_shape=(grid_shape, slot_shape, jax.ShapeDtypeStruct((1, TOK), I32)),
        in_specs=[HBM, VMEM, VMEM, VMEM, VMEM, HBM, HBM, VMEM, SMEM],
        out_specs=(VMEM, VMEM, VMEM),
        scratch_shapes=[pltpu.VMEM((TOK, D), BF16)]
        + qkv_scratch
        + [pltpu.VMEM((HEADS // GROUP, TOK, 128), BF16)],
        compiler_params=pltpu.CompilerParams(vmem_limit_bytes=62 << 20),
        name="dispatch",
    )(x, x1, least, ids, keep.reshape(1, TOK), qkv_weight, proj_weight, attn_gain.reshape(1, D), head_scale)
    slot_buffer = pltpu.VMEM((experts * ROOM, WAYS, LANES), BF16)
    out = pl.pallas_call(
        functools.partial(expert_kernel, experts),
        out_shape=grid_shape,
        in_specs=[HBM, VMEM, VMEM, VMEM, VMEM, VMEM, HBM, HBM],
        out_specs=VMEM,
        scratch_shapes=[
            slot_buffer,
            slot_buffer,
            slot_buffer,
            pltpu.VMEM((8, experts * ROOM // 8, n_tall * hidden), BF16),
            pltpu.VMEM((TOK, D), F32),
            pltpu.VMEM((4, TOK, experts * ROOM // 4), BF16),
            pltpu.VMEM((TOK, 128), F32),
            pltpu.VMEM((n_tall, D, hidden), BF16),
            pltpu.VMEM((n_tall, hidden, D), BF16),
            DMA((2 + n_tall,)),
            DMA((1,)),
            DMA((8,)),
            DMA((1,)),
            DMA((8,)),
            DMA((2,)),
            DMA((2,)),
            DMA((2, n_tall // 2)),
            DMA((2, n_tall // 2)),
        ],
        compiler_params=pltpu.CompilerParams(collective_id=1, has_side_effects=True, vmem_limit_bytes=62 << 20),
        name="experts",
    )(slots, x1, target, ids, router.T, moe_gain.reshape(1, D), w_in, expert_out[0])
    return out.reshape(EDGE, EDGE, D)


def solution(mesh):
    placed = (
        P("tall", "wide", None), P(), P(), P(), P(), P(), P("wide", None, "tall"), P("wide", "tall", None), P(),
        P("tall", "wide", None, None), P("tall", "wide", None),
    )
    return jax.shard_map(
        body, mesh=mesh, in_specs=placed, out_specs=P("tall", "wide", None), check_vma=False
    )
```

time: 131 us -> 105 us (0.80); the launches traced: 131 us -> 103 us
  Pallas kernels: 125 us -> 101 us
  local copies, waits for them, and re-layouts: 5.83 us -> 1.92 us
    pallas_call x1, Pallas kernels: 96.1 us -> 62.3 us  [body(): pl.pallas_call(functools.partial(expert_kernel, experts), out_shape=grid_...]
    pallas_call x1, Pallas kernels: 26.6 us -> 35.6 us  [body(): pl.pallas_call(functools.partial(attention_kernel, limits), out_shape=(gr...]
    unnamed x26 -> x1, local copies, waits for them, and re-layouts: 5.83 us -> 1.92 us
where the time goes in v2:
time: 105 us; the launch traced here: 103 us
  Pallas kernels  101 us (96%)
  local copies, waits for them, and re-layouts  1.92 us (2%)
    pallas_call x1, Pallas kernels, body(): pl.pallas_call(functools.partial(expert_kernel, experts), out_shape=grid_...  62.3 us
    pallas_call x1, Pallas kernels, body(): pl.pallas_call(functools.partial(attention_kernel, limits), out_shape=(gr...  35.6 us
    pallas_call x1, Pallas kernels, body(): pl.pallas_call(functools.partial(dispatch_kernel, limits, experts), out_s...  3.22 us

profile of v2, /device:TPU:1, one launch (start us, length us, event | category | flops | bytes accessed | tf_op | source)
XLA Modules:
  0.0 103.0 jit_solution(5263217285712597633)
XLA Ops:
  0.0 35.6 %attention.1 = (bf16[576,512]{1,0:T(8,128)(2,1)}, bf16[576,512]{1,0:T(8,128)(2,1)}, f32[8,128]{1,0:T(8,128)}, bf16[8,512,256]{2,1,0:T(8,128)(2,1)}) custom-call(bf16[576,512]{1,0:T(8,128)(2,1)} %bitcast.10, bf16[512,1536]{1,0:T(8,128)(2,1)} %qkv_hbm.3, bf16[512,512]{1,0:T(8,128)(2,1)} %proj_hbm.3, f32[1,512]{1,0:T(1,128)} %bitcast.16, f32[16]{0:T(128)} %scale_ref.3, ...), custom_call_target="tpu_custom_call" | custom-call | tf_op jit(solution)/shard_map/attention/pallas_call | solution.py:480
  35.6 3.2 %dispatch.1 = (bf16[576,512]{1,0:T(8,128)(2,1)}, bf16[832,4,128]{2,1,0:T(4,128)(2,1)}, s32[1,576]{1,0:T(1,128)}) custom-call(bf16[576,512]{1,0:T(8,128)(2,1)} %get-tuple-element.12.x_hbm, bf16[576,512]{1,0:T(8,128)(2,1)} %get-tuple-element.13.x1_in, f32[8,128]{1,0:T(8,128)} %get-tuple-element.14.least_ref, s32[1,576]{1,0:T(1,128)} %bitcast.14, ...), custom_call_target="tpu_custom_call" | custom-call | tf_op jit(solution)/shard_map/dispatch/pallas_call | solution.py:495
  38.8 62.3 %experts.1 = bf16[576,512]{1,0:T(8,128)(2,1)} custom-call(bf16[832,4,128]{2,1,0:T(4,128)(2,1)} %get-tuple-element.15.slots_ref, bf16[576,512]{1,0:T(8,128)(2,1)} %get-tuple-element.16.x1_ref, s32[1,576]{1,0:T(1,128)} %get-tuple-element.17.target_ref, s32[1,576]{1,0:T(1,128)} %bitcast.15, bf16[64,512]{1,0:T(8,128)(2,1)} %bitcast.13, f32[1,512]{1,0:T(1,128)} %bitcast.19, ...), custom_call_target="tpu_custom_call" | custom-call | tf_op jit(solution)/shard_map/experts/pallas_call | solution.py:507
  101.1 1.9 %copy.13 = bf16[24,24,512]{2,1,0:T(8,128)(2,1)} copy(bf16[24,24,512]{2,1,0:T(8,128)(2,1)} %bitcast.9) | data formatting | bytes 1179648

commit v3 on v2

v3 whole, which is shorter than its diff:
```python
import functools
import math

import jax
import jax.numpy as jnp
from jax import lax
from jax.experimental import pallas as pl
from jax.experimental.pallas import tpu as pltpu
from jax.sharding import PartitionSpec as P

F32, BF16, I32 = jnp.float32, jnp.bfloat16, jnp.int32
MESH = pl.DeviceIdType.MESH
EDGE = 24
HALF = EDGE // 2
TOK = EDGE * EDGE
QUAD = HALF * HALF
HEADS = 16
HEAD = 32
D = 512
GROUP = 4
SPAN = GROUP * TOK
TILE = 256
LOG2E = math.log2(math.e)
ROOM = 13
LANES = 128
WAYS = D // LANES
NT = (((1,), (1,)), ((), ()))
TN = (((0,), (0,)), ((), ()))
VMEM = pl.BlockSpec(memory_space=pltpu.VMEM)
SMEM = pl.BlockSpec(memory_space=pltpu.SMEM)
HBM = pl.BlockSpec(memory_space=pltpu.HBM)


def dot(a, b, dims=None):
    if dims is None:
        return jnp.dot(a, b, preferred_element_type=F32)
    return lax.dot_general(a, b, dims, preferred_element_type=F32)


def iota(shape, axis):
    return lax.broadcasted_iota(I32, shape, axis)


def norm(value, gain):
    mean = jnp.mean(value, axis=-1, keepdims=True)
    centred = value - mean
    return centred * lax.rsqrt(jnp.mean(centred * centred, axis=-1, keepdims=True) + 1e-5) * gain


def gelu(value):
    return 0.5 * value * (1.0 + lax.erf(value * math.sqrt(0.5)))


def unit(block):
    ones = (iota((TILE, TILE), 0) // HEAD == iota((TILE, TILE), 1) // HEAD).astype(BF16)
    square = block * block
    high = square.astype(BF16)
    low = (square - high.astype(F32)).astype(BF16)
    return (block * lax.rsqrt(dot(high, ones) + dot(low, ones) + 1e-6)).astype(BF16)


def region_column(total_rows, total_cols):
    place = iota((TOK, 1), 0)
    row = lax.axis_index("tall") * EDGE + place // EDGE
    col = lax.axis_index("wide") * EDGE + place % EDGE
    return (row + HALF >= total_rows).astype(I32) * 2 + (col + HALF >= total_cols).astype(I32)


def features(scale_ref, region, q_ref, k_ref, v_ref):
    lane = iota((1, 128), 1)
    feat, own_head = lane % HEAD, lane // HEAD
    key_feat = jnp.where(feat < 12, jnp.where(region == feat % 4, 0.0, -1.0), jnp.where(feat == 12, 1.0, 0.0))
    for g in range(HEADS // GROUP):
        scale = jnp.ones((1, 128), F32)
        for h in range(GROUP):
            scale = jnp.where(own_head == h, scale_ref[g * GROUP + h], scale)
        whole = 100.0 / scale
        high = whole.astype(BF16).astype(F32)
        middle = (whole - high).astype(BF16).astype(F32)
        piece = jnp.where(feat < 4, high, jnp.where(feat < 8, middle, whole - high - middle))
        query_feat = jnp.where(jnp.logical_and(feat < 12, region == feat % 4), piece, 0.0)
        q_ref[g, :, 128:256] = query_feat.astype(BF16)
        for h in range(GROUP):
            mine = own_head == h
            rows = slice(h * TOK, h * TOK + TOK)
            k_ref[g, rows, 128:256] = jnp.where(mine, key_feat, 0.0).astype(BF16)
            v_ref[g, rows, 128:256] = jnp.broadcast_to(jnp.where(mine, 1.0, 0.0), (TOK, 128)).astype(BF16)


def prepare(x, qkv_ref, q_ref, k_ref, v_ref):
    own_head = iota((1, 128), 1) // HEAD
    for half in range(2):
        at = TILE * half
        qn = unit(dot(x, qkv_ref[:, at : at + TILE]))
        kn = unit(dot(x, qkv_ref[:, D + at : D + at + TILE]))
        vb = dot(x, qkv_ref[:, 2 * D + at : 2 * D + at + TILE]).astype(BF16)
        for sub in range(2):
            g = 2 * half + sub
            cut = slice(128 * sub, 128 * sub + 128)
            q_ref[g, :, 0:128] = qn[:, cut]
            for h in range(GROUP):
                mine = own_head == h
                rows = slice(h * TOK, h * TOK + TOK)
                k_ref[g, rows, 0:128] = jnp.where(mine, kn[:, cut], jnp.zeros((), BF16))
                v_ref[g, rows, 0:128] = jnp.where(mine, vb[:, cut], jnp.zeros((), BF16))


def lane_scales(scale_ref, g):
    out = jnp.zeros((1, SPAN), F32)
    for h in range(GROUP):
        out = jnp.where(iota((1, SPAN), 1) // TOK == h, scale_ref[g * GROUP + h] * LOG2E, out)
    return out


def attend(q_ref, k_ref, v_ref, scale_ref, att_ref, between):
    lane = iota((1, 128), 1)
    for g in range(HEADS // GROUP):
        shifted = q_ref[g, :, 128:256]
        for h in range(GROUP):
            score = dot(q_ref[g], k_ref[g, h * TOK : h * TOK + TOK, :], NT)
            peak = jnp.max(score, axis=-1, keepdims=True)
            shifted = jnp.where(lane == h * HEAD + 12, -peak.astype(BF16), shifted)
        q_ref[g, :, 128:256] = shifted
        scales = lane_scales(scale_ref, g)
        acc = None
        for j in range(SPAN // TILE):
            at = slice(TILE * j, TILE * j + TILE)
            powers = jnp.exp2(dot(q_ref[g], k_ref[g, at, :], NT) * scales[:, at]).astype(BF16)
            part = dot(powers, v_ref[g, at, :])
            acc = part if acc is None else acc + part
        att_ref[:, 128 * g : 128 * g + 128] = (acc[:, :128] / acc[:, 128:]).astype(BF16)
        between(g)


def ring_hop(own, gathered, way, step, send_sem, recv_sem):
    tall, wide, n_tall = lax.axis_index("tall"), lax.axis_index("wide"), lax.axis_size("tall")
    owner = lax.rem(tall + n_tall + (1 - step if way == 0 else step - 1), n_tall)
    return pltpu.make_async_remote_copy(
        src_ref=own if step == 1 else gathered.at[owner],
        dst_ref=gathered.at[owner],
        send_sem=send_sem.at[way, step - 1],
        recv_sem=recv_sem.at[way, step - 1],
        device_id=(wide, lax.rem(tall + (1 if way == 0 else n_tall - 1), n_tall)),
        device_id_type=MESH,
    )


def rem(a, n):
    return lax.rem(a, jnp.int32(n))


def div(a, n):
    return lax.div(a, jnp.int32(n))


def partner(k, sign):
    wide = lax.axis_index("wide")
    core, x, y = rem(wide, 2), rem(div(wide, 2), 4), div(wide, 8)
    turn = rem(64 - k, 64)
    step = rem(turn, 8)
    size = div(step + 1, 2)
    dy = size + rem(step + 1, 2) * (8 - 2 * size)
    dx, dc = rem(div(turn, 8), 4), div(turn, 32)
    return (rem(y + 8 + sign * dy, 8) * 4 + rem(x + 4 + sign * dx, 4)) * 2 + rem(core + 2 + sign * dc, 2)


def place_of(expert):
    wide = lax.axis_index("wide")
    dc = (expert % 2 + 2 - wide % 2) % 2
    dx = (expert // 2 % 4 + 4 - wide // 2 % 4) % 4
    dy = (expert // 8 + 8 - wide // 8) % 8
    step = jnp.where(dy == 0, 0, jnp.where(dy <= 4, 2 * dy - 1, 16 - 2 * dy))
    return (64 - (dc * 32 + dx * 8 + step)) % 64


def block_kernel(
    limits, experts,
    tokens_hbm, qkv_hbm, proj_hbm, attn_gain_ref, scale_ref, router_ref, in_hbm, out_hbm, moe_gain_ref, ids_ref, keep_ref,
    result_ref,
    tokens_ref, send, recv, qkv_ref, proj_ref, q_ref, k_ref, v_ref, att_ref, x_ref, x1_ref,
    scatter, gather, slots, arrived, made, back, hidden, gate, picked, w_in, w_out,
    load_sem, own_sem, send_sem, recv_sem, in_send, in_recv, out_send, out_recv, give_send, give_recv, take_send, take_recv,
):
    tall, wide = lax.axis_index("tall"), lax.axis_index("wide")
    n_tall, n_wide = lax.axis_size("tall"), lax.axis_size("wide")
    last = n_tall // 2
    loads = [
        pltpu.make_async_copy(tokens_hbm, tokens_ref, load_sem.at[0]),
        pltpu.make_async_copy(qkv_hbm, qkv_ref, load_sem.at[1]),
        pltpu.make_async_copy(proj_hbm, proj_ref, load_sem.at[2]),
        pltpu.make_async_copy(in_hbm, w_in.at[tall], load_sem.at[3]),
        pltpu.make_async_copy(out_hbm, w_out.at[tall], load_sem.at[4]),
    ]
    for load in loads:
        load.start()

    up, left = lax.rem(tall + n_tall - 1, n_tall), lax.rem(wide + n_wide - 1, n_wide)
    down, right = lax.rem(tall + 1, n_tall), lax.rem(wide + 1, n_wide)
    barrier = pltpu.get_barrier_semaphore()
    for peer in ((wide, up), (wide, down), (left, up), (right, down)):
        pl.semaphore_signal(barrier, inc=1, device_id=peer, device_id_type=MESH)

    def greet(k, carry):
        pl.semaphore_signal(barrier, inc=1, device_id=(rem(wide + k, n_wide), tall), device_id_type=MESH)
        return carry

    lax.fori_loop(1, n_wide, greet, 0)

    place = iota((TOK, TOK), 0)
    quad, rest = place // QUAD, place % QUAD
    row = rest // HALF + jnp.where(quad % 2 == 0, HALF, 0)
    col = rest % HALF + jnp.where(quad < 2, HALF, 0)
    pick = (iota((TOK, TOK), 1) == row * EDGE + col).astype(BF16)
    loads[0].wait()
    send[...] = dot(pick, tokens_ref[...]).astype(BF16)
    recv[0:QUAD, :] = send[0:QUAD, :]
    pl.semaphore_wait(barrier, n_wide + 3)
    copies = []
    for i, peer in enumerate([(wide, up), (left, tall), (left, up)]):
        rows = pl.ds(QUAD * (i + 1), QUAD)
        copies.append(
            pltpu.make_async_remote_copy(
                src_ref=send.at[rows], dst_ref=recv.at[rows], send_sem=send_sem.at[i], recv_sem=recv_sem.at[i],
                device_id=peer, device_id_type=MESH,
            )
        )
        copies[-1].start()

    hops = {}

    def launch(way, step):
        started = []
        if step < last or way == 0:
            started.append(ring_hop(in_hbm, w_in, way, step, in_send, in_recv))
        if step < last:
            started.append(ring_hop(out_hbm, w_out, way, step, out_send, out_recv))
        else:
            owner = lax.rem(tall + (n_tall + 1 - last if way == 0 else last - 1), n_tall)
            rows = pl.ds(TILE // 2 * way, TILE // 2)
            started.append(
                pltpu.make_async_remote_copy(
                    src_ref=w_out.at[owner, rows], dst_ref=w_out.at[owner, rows], send_sem=out_send.at[way, last - 1],
                    recv_sem=out_recv.at[way, last - 1], device_id=(wide, down if way == 0 else up),
                    device_id_type=MESH,
                )
            )
        for copy in started:
            copy.start()
        hops[way, step] = started

    def arrive(way, step):
        for copy in hops[way, step]:
            copy.wait_recv()

    def onward(way, step):
        arrive(way, step)
        launch(way, step + 1)

    launch(0, 1)

    per = 8
    groups = n_wide // per
    room = per * ROOM
    span = 2 * room
    ids, kept = ids_ref[...], keep_ref[...] == 1
    named = iota((experts, TOK), 0) == ids
    live = jnp.where(jnp.logical_and(named, kept), 1.0, 0.0)
    earlier = (iota((TOK, TOK), 0) < iota((TOK, TOK), 1)).astype(BF16)
    slot = jnp.sum(jnp.where(named, dot(live.astype(BF16), earlier), 0.0), axis=0, keepdims=True)
    target = jnp.where(kept, place_of(ids) * ROOM + slot.astype(I32), -1)
    scatter[...] = (iota((experts * ROOM, TOK), 0) == target).astype(BF16)
    eye = (iota((experts, experts), 0) == iota((experts, experts), 1)).astype(BF16)
    chosen = dot(live.astype(BF16), eye, TN)
    slot = jnp.sum(dot((live * slot).astype(BF16), eye, TN), axis=-1, keepdims=True)
    block = jnp.sum(chosen * place_of(iota((1, experts), 1)).astype(F32), axis=-1, keepdims=True)
    in_use = jnp.sum(chosen, axis=-1, keepdims=True)
    landing = jnp.where(in_use > 0.5, block * ROOM + slot, -1.0).astype(I32)
    for pair in range(groups // 2):
        gather[pair] = (iota((TOK, span), 1) + pair * span == landing).astype(BF16)

    features(scale_ref, region_column(*limits), q_ref, k_ref, v_ref)
    row, col = place // EDGE, place % EDGE
    quad = (row // HALF) + 2 * (col // HALF)
    pick = (iota((TOK, TOK), 1) == quad * QUAD + (row % HALF) * HALF + col % HALF).astype(BF16)
    for load in loads[1:]:
        load.wait()
    for copy in copies:
        copy.wait()
    launch(1, 1)
    x = dot(pick, recv[...]).astype(BF16)
    x_ref[...] = x
    prepare(x, qkv_ref, q_ref, k_ref, v_ref)

    def between(g):
        if g == 1:
            onward(0, 1)
        if g == 3:
            onward(1, 1)

    attend(q_ref, k_ref, v_ref, scale_ref, att_ref, between)
    out = dot(att_ref[...], proj_ref[...])
    x1_ref[...] = (x_ref[...].astype(F32) + norm(out, attn_gain_ref[...])).astype(BF16)

    def exchange(source, landing, send_sem, recv_sem, sign, group):
        def one(k, carry):
            rows = pl.ds(k * ROOM, ROOM)
            pltpu.make_async_remote_copy(
                src_ref=source.at[rows], dst_ref=landing.at[rows], send_sem=send_sem, recv_sem=recv_sem.at[group],
                device_id=(partner(k, sign), tall), device_id_type=MESH,
            ).start()
            return carry

        lax.fori_loop(max(1, group * per), group * per + per, one, 0)

    def whole_of(ref, blocks, send_sem, recv_sem):
        rows = pl.ds(0, blocks * ROOM)
        return pltpu.make_async_remote_copy(
            src_ref=ref.at[rows], dst_ref=ref.at[rows], send_sem=send_sem, recv_sem=recv_sem,
            device_id=(wide, down), device_id_type=MESH,
        )

    for pair in range(groups // 2):
        rows = slice(pair * span, pair * span + span)
        slots[rows] = dot(scatter[rows, :], x1_ref[...]).astype(BF16).reshape(span, WAYS, LANES)
        for group in (2 * pair, 2 * pair + 1):
            exchange(slots, arrived, give_send.at[0], give_recv, 1, group)
    arrived[0:ROOM] = slots[0:ROOM]
    onward(0, 2)
    logit = jnp.sum(dot(x1_ref[...], router_ref[...], NT) * chosen, axis=-1, keepdims=True)
    gate[...] = jnp.broadcast_to(in_use * jax.nn.sigmoid(logit), gate.shape)
    onward(1, 2)
    onward(0, 3)
    onward(1, 3)
    arrive(0, last)
    arrive(1, last)
    for group in range(groups):
        rows = slice(group * room, group * room + room)
        whole_of(arrived, per - (group == 0), give_send.at[0], give_recv.at[group]).wait_recv()
        here = arrived[rows].reshape(room, D)
        for c in range(n_tall):
            hidden[:, c * TILE : c * TILE + TILE] = gelu(dot(here, w_in[c])).astype(BF16)
        out = dot(hidden[...], w_out[...].reshape(n_tall * TILE, D)).astype(BF16)
        made[rows] = out.reshape(room, WAYS, LANES)
        exchange(made, back, take_send.at[0], take_recv, -1, group)
    back[0:ROOM] = made[0:ROOM]
    for started in hops.values():
        for copy in started:
            copy.wait_send()
    whole_of(slots, n_wide - 1, give_send.at[0], give_recv.at[0]).wait_send()
    for pair in range(groups // 2):
        for group in (2 * pair, 2 * pair + 1):
            whole_of(back, per - (group == 0), take_send.at[0], take_recv.at[group]).wait_recv()
        part = dot(gather[pair], back[pair * span : pair * span + span].reshape(span, D))
        if pair < groups // 2 - 1:
            picked[...] = part if pair == 0 else picked[...] + part
    result_ref[...] = (
        x1_ref[...].astype(F32) + gate[:, 0:1] * norm(picked[...] + part, moe_gain_ref[...])
    ).astype(BF16)
    whole_of(made, n_wide - 1, take_send.at[0], take_recv.at[0]).wait_send()


def body(
    tokens, qkv_weight, proj_weight, head_scale, attn_gain, router, expert_in, expert_out, moe_gain, expert_ids, keep
):
    n_tall, n_wide = lax.axis_size("tall"), lax.axis_size("wide")
    experts = router.shape[1]
    limits = (EDGE * n_tall, EDGE * n_wide)
    hidden = expert_in.shape[2]
    rows = pltpu.VMEM((TOK, D), BF16)
    slot_buffer = pltpu.VMEM((experts * ROOM, WAYS, LANES), BF16)
    DMA = pltpu.SemaphoreType.DMA
    ring_sem = DMA((2, n_tall // 2))
    out = pl.pallas_call(
        functools.partial(block_kernel, limits, experts),
        out_shape=jax.ShapeDtypeStruct((TOK, D), BF16),
        in_specs=[HBM, HBM, HBM, VMEM, SMEM, VMEM, HBM, HBM, VMEM, VMEM, VMEM],
        out_specs=VMEM,
        scratch_shapes=[
            rows, rows, rows,
            pltpu.VMEM((D, 3 * D), BF16),
            pltpu.VMEM((D, D), BF16),
            pltpu.VMEM((HEADS // GROUP, TOK, TILE), BF16),
            pltpu.VMEM((HEADS // GROUP, SPAN, TILE), BF16),
            pltpu.VMEM((HEADS // GROUP, SPAN, TILE), BF16),
            rows, rows, rows,
            pltpu.VMEM((experts * ROOM, TOK), BF16),
            pltpu.VMEM((4, TOK, experts * ROOM // 4), BF16),
            slot_buffer, slot_buffer, slot_buffer, slot_buffer,
            pltpu.VMEM((experts * ROOM // 8, n_tall * hidden), BF16),
            pltpu.VMEM((TOK, 128), F32),
            pltpu.VMEM((TOK, D), F32),
            pltpu.VMEM((n_tall, D, hidden), BF16),
            pltpu.VMEM((n_tall, hidden, D), BF16),
            DMA((5,)), DMA((1,)), DMA((3,)), DMA((3,)), ring_sem, ring_sem, ring_sem, ring_sem,
            DMA((1,)), DMA((8,)), DMA((1,)), DMA((8,)),
        ],
        compiler_params=pltpu.CompilerParams(collective_id=0, has_side_effects=True, vmem_limit_bytes=62 << 20),
        name="block",
    )(
        tokens.reshape(TOK, D), qkv_weight, proj_weight, attn_gain.reshape(1, D), head_scale, router.T, expert_in[0],
        expert_out[0], moe_gain.reshape(1, D), expert_ids.reshape(1, TOK), keep.reshape(1, TOK),
    )
    return out.reshape(EDGE, EDGE, D)


def solution(mesh):
    placed = (
        P("tall", "wide", None), P(), P(), P(), P(), P(), P("wide", None, "tall"), P("wide", "tall", None), P(),
        P("tall", "wide", None, None), P("tall", "wide", None),
    )
    return jax.shard_map(
        body, mesh=mesh, in_specs=placed, out_specs=P("tall", "wide", None), check_vma=False
    )
```

time: 105 us -> 93.4 us (0.89)
  Pallas kernels: 101 us -> 89.7 us
    pallas_call x3 -> x1, Pallas kernels: 101 us -> 89.7 us  [body(): pl.pallas_call(functools.partial(block_kernel, limits, experts), out_shap...]
where the time goes in v3:
time: 93.4 us; the launch traced here: 91.6 us
  Pallas kernels  89.7 us (96%)
  local copies, waits for them, and re-layouts  1.92 us (2%)
    pallas_call x1, Pallas kernels, body(): pl.pallas_call(functools.partial(block_kernel, limits, experts), out_shap...  89.7 us
    unnamed x1, local copies, waits for them, and re-layouts  1.92 us

profile of v3, /device:TPU:1, one launch (start us, length us, event | category | flops | bytes accessed | tf_op | source)
XLA Modules:
  0.0 91.6 jit_solution(11326560967316646487)
XLA Ops:
  0.0 89.7 %block.1 = bf16[576,512]{1,0:T(8,128)(2,1)} custom-call(bf16[576,512]{1,0:T(8,128)(2,1)} %bitcast.10, bf16[512,1536]{1,0:T(8,128)(2,1)} %qkv_hbm.1, bf16[512,512]{1,0:T(8,128)(2,1)} %proj_hbm.1, f32[1,512]{1,0:T(1,128)} %bitcast.16, f32[16]{0:T(128)} %scale_ref.1, bf16[64,512]{1,0:T(8,128)(2,1)} %bitcast.13, bf16[512,256]{1,0:T(8,128)(2,1)} %bitcast.11, ...), custom_call_target="tpu_custom_call" | custom-call | tf_op jit(solution)/shard_map/block/pallas_call | solution.py:373
  89.7 1.9 %copy.13 = bf16[24,24,512]{2,1,0:T(8,128)(2,1)} copy(bf16[24,24,512]{2,1,0:T(8,128)(2,1)} %bitcast.9) | data formatting | bytes 1179648

commit v4 on v3

--- a/solution.py
+++ b/solution.py
@@ -23,6 +23,8 @@
 LOG2E = math.log2(math.e)
 ROOM = 13
 LANES = 128
+TRIPLE = 3
+THIRD = TOK // TRIPLE
 WAYS = D // LANES
 NT = (((1,), (1,)), ((), ()))
 TN = (((0,), (0,)), ((), ()))
@@ -59,17 +61,18 @@
     return (block * lax.rsqrt(dot(high, ones) + dot(low, ones) + 1e-6)).astype(BF16)
 
 
-def region_column(total_rows, total_cols):
-    place = iota((TOK, 1), 0)
+def region_column(total_rows, total_cols, stride=1):
+    place = iota((TOK // stride, 1), 0) * stride
     row = lax.axis_index("tall") * EDGE + place // EDGE
     col = lax.axis_index("wide") * EDGE + place % EDGE
     return (row + HALF >= total_rows).astype(I32) * 2 + (col + HALF >= total_cols).astype(I32)
 
 
-def features(scale_ref, region, q_ref, k_ref, v_ref):
+def features(scale_ref, region, region3, q_ref, k_ref, k3_ref, v_ref):
     lane = iota((1, 128), 1)
     feat, own_head = lane % HEAD, lane // HEAD
     key_feat = jnp.where(feat < 12, jnp.where(region == feat % 4, 0.0, -1.0), jnp.where(feat == 12, 1.0, 0.0))
+    key3_feat = jnp.where(jnp.logical_and(feat < 12, region3 != feat % 4), -1.0, 0.0)
     for g in range(HEADS // GROUP):
         scale = jnp.ones((1, 128), F32)
         for h in range(GROUP):
@@ -84,15 +87,18 @@
             mine = own_head == h
             rows = slice(h * TOK, h * TOK + TOK)
             k_ref[g, rows, 128:256] = jnp.where(mine, key_feat, 0.0).astype(BF16)
+            k3_ref[g, h * THIRD : h * THIRD + THIRD, 128:256] = jnp.where(mine, key3_feat, 0.0).astype(BF16)
             v_ref[g, rows, 128:256] = jnp.broadcast_to(jnp.where(mine, 1.0, 0.0), (TOK, 128)).astype(BF16)
 
 
-def prepare(x, qkv_ref, q_ref, k_ref, v_ref):
+def prepare(x, qkv_ref, q_ref, k_ref, k3_ref, v_ref):
     own_head = iota((1, 128), 1) // HEAD
+    thirds = (iota((THIRD, TOK), 1) // TRIPLE == iota((THIRD, TOK), 0)).astype(BF16)
     for half in range(2):
         at = TILE * half
         qn = unit(dot(x, qkv_ref[:, at : at + TILE]))
         kn = unit(dot(x, qkv_ref[:, D + at : D + at + TILE]))
+        k3 = (dot(thirds, kn) * (1.0 / TRIPLE)).astype(BF16)
         vb = dot(x, qkv_ref[:, 2 * D + at : 2 * D + at + TILE]).astype(BF16)
         for sub in range(2):
             g = 2 * half + sub
@@ -102,6 +108,7 @@
                 mine = own_head == h
                 rows = slice(h * TOK, h * TOK + TOK)
                 k_ref[g, rows, 0:128] = jnp.where(mine, kn[:, cut], jnp.zeros((), BF16))
+                k3_ref[g, h * THIRD : h * THIRD + THIRD, 0:128] = jnp.where(mine, k3[:, cut], jnp.zeros((), BF16))
                 v_ref[g, rows, 0:128] = jnp.where(mine, vb[:, cut], jnp.zeros((), BF16))
 
 
@@ -112,14 +119,24 @@
     return out
 
 
-def attend(q_ref, k_ref, v_ref, scale_ref, att_ref, between):
+def attend(q_ref, k_ref, k3_ref, v_ref, scale_ref, att_ref, between):
     lane = iota((1, 128), 1)
     for g in range(HEADS // GROUP):
         shifted = q_ref[g, :, 128:256]
+        score = dot(q_ref[g], k3_ref[g], NT)
+        tops = [None] * GROUP
+        for n in range(GROUP * THIRD // 128):
+            piece = score[:, 128 * n : 128 * n + 128]
+            low, high = 128 * n // THIRD, (128 * n + 127) // THIRD
+            edge = high * THIRD - 128 * n
+            for h in range(low, high + 1):
+                part = piece
+                if low != high:
+                    part = jnp.where((lane < edge) if h == low else (lane >= edge), piece, -jnp.inf)
+                tops[h] = part if tops[h] is None else jnp.maximum(tops[h], part)
         for h in range(GROUP):
-            score = dot(q_ref[g], k_ref[g, h * TOK : h * TOK + TOK, :], NT)
-            peak = jnp.max(score, axis=-1, keepdims=True)
-            shifted = jnp.where(lane == h * HEAD + 12, -peak.astype(BF16), shifted)
+            shift = -(jnp.max(tops[h], axis=-1, keepdims=True) + 2.0 / 3.0)
+            shifted = jnp.where(lane == h * HEAD + 12, shift.astype(BF16), shifted)
         q_ref[g, :, 128:256] = shifted
         scales = lane_scales(scale_ref, g)
         acc = None
@@ -177,9 +194,9 @@
     limits, experts,
     tokens_hbm, qkv_hbm, proj_hbm, attn_gain_ref, scale_ref, router_ref, in_hbm, out_hbm, moe_gain_ref, ids_ref, keep_ref,
     result_ref,
-    tokens_ref, send, recv, qkv_ref, proj_ref, q_ref, k_ref, v_ref, att_ref, x_ref, x1_ref,
+    tokens_ref, send, recv, qkv_ref, proj_ref, q_ref, k_ref, k3_ref, v_ref, att_ref, x_ref, x1_ref,
     scatter, gather, slots, arrived, made, back, hidden, gate, picked, w_in, w_out,
-    load_sem, own_sem, send_sem, recv_sem, in_send, in_recv, out_send, out_recv, give_send, give_recv, take_send, take_recv,
+    load_sem, line_sem, send_sem, recv_sem, in_send, in_recv, out_send, out_recv, give_send, give_recv, take_send, take_recv,
 ):
     tall, wide = lax.axis_index("tall"), lax.axis_index("wide")
     n_tall, n_wide = lax.axis_size("tall"), lax.axis_size("wide")
@@ -197,14 +214,12 @@
     up, left = lax.rem(tall + n_tall - 1, n_tall), lax.rem(wide + n_wide - 1, n_wide)
     down, right = lax.rem(tall + 1, n_tall), lax.rem(wide + 1, n_wide)
     barrier = pltpu.get_barrier_semaphore()
-    for peer in ((wide, up), (wide, down), (left, up), (right, down)):
+    near = [(wide, up), (wide, down), (left, up), (right, down), (left, tall), (right, tall)]
+    row_start, row_place = div(wide, 8) * 8, rem(wide, 8)
+    across = [(rem(wide + 8 * i, n_wide), tall) for i in range(1, 8)]
+    near += across + [(row_start + rem(row_place + i, 8), tall) for i in range(1, 8)]
+    for peer in near:
         pl.semaphore_signal(barrier, inc=1, device_id=peer, device_id_type=MESH)
-
-    def greet(k, carry):
-        pl.semaphore_signal(barrier, inc=1, device_id=(rem(wide + k, n_wide), tall), device_id_type=MESH)
-        return carry
-
-    lax.fori_loop(1, n_wide, greet, 0)
 
     place = iota((TOK, TOK), 0)
     quad, rest = place // QUAD, place % QUAD
@@ -214,7 +229,7 @@
     loads[0].wait()
     send[...] = dot(pick, tokens_ref[...]).astype(BF16)
     recv[0:QUAD, :] = send[0:QUAD, :]
-    pl.semaphore_wait(barrier, n_wide + 3)
+    pl.semaphore_wait(barrier, len(near))
     copies = []
     for i, peer in enumerate([(wide, up), (left, tall), (left, up)]):
         rows = pl.ds(QUAD * (i + 1), QUAD)
@@ -228,35 +243,29 @@
 
     hops = {}
 
-    def launch(way, step):
-        started = []
-        if step < last or way == 0:
-            started.append(ring_hop(in_hbm, w_in, way, step, in_send, in_recv))
-        if step < last:
-            started.append(ring_hop(out_hbm, w_out, way, step, out_send, out_recv))
+    def launch(kind, way, step):
+        if step < last or (kind == 0 and way == 0):
+            if kind == 0:
+                copy = ring_hop(in_hbm, w_in, way, step, in_send, in_recv)
+            else:
+                copy = ring_hop(out_hbm, w_out, way, step, out_send, out_recv)
         else:
             owner = lax.rem(tall + (n_tall + 1 - last if way == 0 else last - 1), n_tall)
             rows = pl.ds(TILE // 2 * way, TILE // 2)
-            started.append(
-                pltpu.make_async_remote_copy(
-                    src_ref=w_out.at[owner, rows], dst_ref=w_out.at[owner, rows], send_sem=out_send.at[way, last - 1],
-                    recv_sem=out_recv.at[way, last - 1], device_id=(wide, down if way == 0 else up),
-                    device_id_type=MESH,
-                )
+            copy = pltpu.make_async_remote_copy(
+                src_ref=w_out.at[owner, rows], dst_ref=w_out.at[owner, rows], send_sem=out_send.at[way, last - 1],
+                recv_sem=out_recv.at[way, last - 1], device_id=(wide, down if way == 0 else up), device_id_type=MESH,
             )
-        for copy in started:
-            copy.start()
-        hops[way, step] = started
-
-    def arrive(way, step):
-        for copy in hops[way, step]:
-            copy.wait_recv()
-
-    def onward(way, step):
-        arrive(way, step)
-        launch(way, step + 1)
-
-    launch(0, 1)
+        copy.start()
+        hops[kind, way, step] = copy
+
+    def onward(kind, way, step):
+        hops[kind, way, step].wait_recv()
+        launch(kind, way, step + 1)
+
+    launch(0, 0, 1)
+    for peer in across:
+        pl.semaphore_signal(line_sem, inc=1, device_id=peer, device_id_type=MESH)
 
     per = 8
     groups = n_wide // per
@@ -278,7 +287,8 @@
     for pair in range(groups // 2):
         gather[pair] = (iota((TOK, span), 1) + pair * span == landing).astype(BF16)
 
-    features(scale_ref, region_column(*limits), q_ref, k_ref, v_ref)
+    launch(1, 0, 1)
+    features(scale_ref, region_column(*limits), region_column(*limits, TRIPLE), q_ref, k_ref, k3_ref, v_ref)
     row, col = place // EDGE, place % EDGE
     quad = (row // HALF) + 2 * (col // HALF)
     pick = (iota((TOK, TOK), 1) == quad * QUAD + (row % HALF) * HALF + col % HALF).astype(BF16)
@@ -286,20 +296,20 @@
         load.wait()
     for copy in copies:
         copy.wait()
-    launch(1, 1)
+    launch(0, 1, 1)
     x = dot(pick, recv[...]).astype(BF16)
     x_ref[...] = x
-    prepare(x, qkv_ref, q_ref, k_ref, v_ref)
+    prepare(x, qkv_ref, q_ref, k_ref, k3_ref, v_ref)
+    launch(1, 1, 1)
 
     def between(g):
-        if g == 1:
-            onward(0, 1)
-        if g == 3:
-            onward(1, 1)
-
-    attend(q_ref, k_ref, v_ref, scale_ref, att_ref, between)
+        for kind, way, step in (((0, 0, 1),), ((1, 0, 1),), ((0, 1, 1),), ((1, 1, 1), (0, 0, 2)))[g]:
+            onward(kind, way, step)
+
+    attend(q_ref, k_ref, k3_ref, v_ref, scale_ref, att_ref, between)
     out = dot(att_ref[...], proj_ref[...])
     x1_ref[...] = (x_ref[...].astype(F32) + norm(out, attn_gain_ref[...])).astype(BF16)
+    pl.semaphore_wait(line_sem, len(across))
 
     def exchange(source, landing, send_sem, recv_sem, sign, group):
         def one(k, carry):
@@ -324,28 +334,31 @@
         slots[rows] = dot(scatter[rows, :], x1_ref[...]).astype(BF16).reshape(span, WAYS, LANES)
         for group in (2 * pair, 2 * pair + 1):
             exchange(slots, arrived, give_send.at[0], give_recv, 1, group)
+        if pair > 0:
+            onward(*((1, 0, 2), (0, 1, 2), (1, 1, 2))[pair - 1])
     arrived[0:ROOM] = slots[0:ROOM]
-    onward(0, 2)
     logit = jnp.sum(dot(x1_ref[...], router_ref[...], NT) * chosen, axis=-1, keepdims=True)
     gate[...] = jnp.broadcast_to(in_use * jax.nn.sigmoid(logit), gate.shape)
-    onward(1, 2)
-    onward(0, 3)
-    onward(1, 3)
-    arrive(0, last)
-    arrive(1, last)
+    onward(0, 0, 3)
+    onward(1, 0, 3)
+    hops[0, 1, 3].wait_recv()
+    onward(1, 1, 3)
+    hops[0, 0, last].wait_recv()
     for group in range(groups):
         rows = slice(group * room, group * room + room)
         whole_of(arrived, per - (group == 0), give_send.at[0], give_recv.at[group]).wait_recv()
         here = arrived[rows].reshape(room, D)
         for c in range(n_tall):
             hidden[:, c * TILE : c * TILE + TILE] = gelu(dot(here, w_in[c])).astype(BF16)
+        if group == 0:
+            hops[1, 0, last].wait_recv()
+            hops[1, 1, last].wait_recv()
         out = dot(hidden[...], w_out[...].reshape(n_tall * TILE, D)).astype(BF16)
         made[rows] = out.reshape(room, WAYS, LANES)
         exchange(made, back, take_send.at[0], take_recv, -1, group)
     back[0:ROOM] = made[0:ROOM]
-    for started in hops.values():
-        for copy in started:
-            copy.wait_send()
+    for copy in hops.values():
+        copy.wait_send()
     whole_of(slots, n_wide - 1, give_send.at[0], give_recv.at[0]).wait_send()
     for pair in range(groups // 2):
         for group in (2 * pair, 2 * pair + 1):
@@ -381,6 +394,7 @@
             pltpu.VMEM((D, D), BF16),
             pltpu.VMEM((HEADS // GROUP, TOK, TILE), BF16),
             pltpu.VMEM((HEADS // GROUP, SPAN, TILE), BF16),
+            pltpu.VMEM((HEADS // GROUP, GROUP * THIRD, TILE), BF16),
             pltpu.VMEM((HEADS // GROUP, SPAN, TILE), BF16),
             rows, rows, rows,
             pltpu.VMEM((experts * ROOM, TOK), BF16),
@@ -391,7 +405,7 @@
             pltpu.VMEM((TOK, D), F32),
             pltpu.VMEM((n_tall, D, hidden), BF16),
             pltpu.VMEM((n_tall, hidden, D), BF16),
-            DMA((5,)), DMA((1,)), DMA((3,)), DMA((3,)), ring_sem, ring_sem, ring_sem, ring_sem,
+            DMA((5,)), pltpu.SemaphoreType.REGULAR, DMA((3,)), DMA((3,)), ring_sem, ring_sem, ring_sem, ring_sem,
             DMA((1,)), DMA((8,)), DMA((1,)), DMA((8,)),
         ],
         compiler_params=pltpu.CompilerParams(collective_id=0, has_side_effects=True, vmem_limit_bytes=62 << 20),

time: 93.4 us -> 87.8 us (0.940)
  the two profiles are of different devices: /device:TPU:1 before, /device:TPU:2 now
where the time goes in v4:
time: 87.8 us; the launch traced here: 87.6 us
  Pallas kernels  85.7 us (98%)
  local copies, waits for them, and re-layouts  1.92 us (2%)
    pallas_call x1, Pallas kernels, body(): pl.pallas_call(functools.partial(block_kernel, limits, experts), out_shap...  85.7 us
    unnamed x1, local copies, waits for them, and re-layouts  1.92 us

profile of v4, /device:TPU:2, one launch (start us, length us, event | category | flops | bytes accessed | tf_op | source)
XLA Modules:
  0.0 87.6 jit_solution(7688294661433022389)
XLA Ops:
  0.0 85.7 %block.1 = bf16[576,512]{1,0:T(8,128)(2,1)} custom-call(bf16[576,512]{1,0:T(8,128)(2,1)} %bitcast.10, bf16[512,1536]{1,0:T(8,128)(2,1)} %qkv_hbm.1, bf16[512,512]{1,0:T(8,128)(2,1)} %proj_hbm.1, f32[1,512]{1,0:T(1,128)} %bitcast.16, f32[16]{0:T(128)} %scale_ref.1, bf16[64,512]{1,0:T(8,128)(2,1)} %bitcast.13, bf16[512,256]{1,0:T(8,128)(2,1)} %bitcast.11, ...), custom_call_target="tpu_custom_call" | custom-call | tf_op jit(solution)/shard_map/block/pallas_call | solution.py:386
  85.7 1.9 %copy.13 = bf16[24,24,512]{2,1,0:T(8,128)(2,1)} copy(bf16[24,24,512]{2,1,0:T(8,128)(2,1)} %bitcast.9) | data formatting | bytes 1179648

commit v5 on v4

--- a/solution.py
+++ b/solution.py
@@ -206,7 +206,8 @@
         pltpu.make_async_copy(qkv_hbm, qkv_ref, load_sem.at[1]),
         pltpu.make_async_copy(proj_hbm, proj_ref, load_sem.at[2]),
         pltpu.make_async_copy(in_hbm, w_in.at[tall], load_sem.at[3]),
-        pltpu.make_async_copy(out_hbm, w_out.at[tall], load_sem.at[4]),
+        pltpu.make_async_copy(out_hbm.at[:, pl.ds(0, TILE)], w_out.at[0, tall], load_sem.at[4]),
+        pltpu.make_async_copy(out_hbm.at[:, pl.ds(TILE, TILE)], w_out.at[1, tall], load_sem.at[5]),
     ]
     for load in loads:
         load.start()
@@ -244,17 +245,20 @@
     hops = {}
 
     def launch(kind, way, step):
-        if step < last or (kind == 0 and way == 0):
-            if kind == 0:
-                copy = ring_hop(in_hbm, w_in, way, step, in_send, in_recv)
-            else:
-                copy = ring_hop(out_hbm, w_out, way, step, out_send, out_recv)
+        if kind == 0:
+            copy = ring_hop(in_hbm, w_in, way, step, in_send, in_recv)
+        elif step < last:
+            copy = ring_hop(
+                out_hbm.at[:, pl.ds(TILE * (kind - 1), TILE)], w_out.at[kind - 1], way, step,
+                out_send.at[kind - 1], out_recv.at[kind - 1],
+            )
         else:
             owner = lax.rem(tall + (n_tall + 1 - last if way == 0 else last - 1), n_tall)
-            rows = pl.ds(TILE // 2 * way, TILE // 2)
+            block = w_out.at[kind - 1, owner, pl.ds(TILE // 2 * way, TILE // 2)]
             copy = pltpu.make_async_remote_copy(
-                src_ref=w_out.at[owner, rows], dst_ref=w_out.at[owner, rows], send_sem=out_send.at[way, last - 1],
-                recv_sem=out_recv.at[way, last - 1], device_id=(wide, down if way == 0 else up), device_id_type=MESH,
+                src_ref=block, dst_ref=block, send_sem=out_send.at[kind - 1, way, last - 1],
+                recv_sem=out_recv.at[kind - 1, way, last - 1], device_id=(wide, down if way == 0 else up),
+                device_id_type=MESH,
             )
         copy.start()
         hops[kind, way, step] = copy
@@ -305,6 +309,8 @@
     def between(g):
         for kind, way, step in (((0, 0, 1),), ((1, 0, 1),), ((0, 1, 1),), ((1, 1, 1), (0, 0, 2)))[g]:
             onward(kind, way, step)
+        if g % 2:
+            launch(2, g // 2, 1)
 
     attend(q_ref, k_ref, k3_ref, v_ref, scale_ref, att_ref, between)
     out = dot(att_ref[...], proj_ref[...])
@@ -315,7 +321,7 @@
         def one(k, carry):
             rows = pl.ds(k * ROOM, ROOM)
             pltpu.make_async_remote_copy(
-                src_ref=source.at[rows], dst_ref=landing.at[rows], send_sem=send_sem, recv_sem=recv_sem.at[group],
+                src_ref=source.at[rows], dst_ref=landing.at[rows], send_sem=send_sem, recv_sem=recv_sem,
                 device_id=(partner(k, sign), tall), device_id_type=MESH,
             ).start()
             return carry
@@ -333,43 +339,61 @@
         rows = slice(pair * span, pair * span + span)
         slots[rows] = dot(scatter[rows, :], x1_ref[...]).astype(BF16).reshape(span, WAYS, LANES)
         for group in (2 * pair, 2 * pair + 1):
-            exchange(slots, arrived, give_send.at[0], give_recv, 1, group)
+            exchange(slots, arrived, give_send.at[0], give_recv.at[group], 1, group)
         if pair > 0:
-            onward(*((1, 0, 2), (0, 1, 2), (1, 1, 2))[pair - 1])
+            for kind, way, step in (((1, 0, 2),), ((0, 1, 2), (2, 0, 1)), ((1, 1, 2), (2, 1, 1)))[pair - 1]:
+                onward(kind, way, step)
     arrived[0:ROOM] = slots[0:ROOM]
     logit = jnp.sum(dot(x1_ref[...], router_ref[...], NT) * chosen, axis=-1, keepdims=True)
     gate[...] = jnp.broadcast_to(in_use * jax.nn.sigmoid(logit), gate.shape)
     onward(0, 0, 3)
     onward(1, 0, 3)
+    onward(2, 0, 2)
     hops[0, 1, 3].wait_recv()
     onward(1, 1, 3)
+    onward(2, 1, 2)
     hops[0, 0, last].wait_recv()
+
+    def finish(half, group):
+        rows = slice(group * room, group * room + room)
+        out = dot(hidden[group], w_out[half].reshape(n_tall * TILE, TILE)).astype(BF16)
+        made[half, rows] = out.reshape(room, WAYS // 2, LANES)
+        exchange(made.at[half], back.at[half], take_send.at[half], take_recv.at[half, group], -1, group)
+
     for group in range(groups):
         rows = slice(group * room, group * room + room)
         whole_of(arrived, per - (group == 0), give_send.at[0], give_recv.at[group]).wait_recv()
         here = arrived[rows].reshape(room, D)
         for c in range(n_tall):
-            hidden[:, c * TILE : c * TILE + TILE] = gelu(dot(here, w_in[c])).astype(BF16)
+            hidden[group, :, c * TILE : c * TILE + TILE] = gelu(dot(here, w_in[c])).astype(BF16)
         if group == 0:
             hops[1, 0, last].wait_recv()
             hops[1, 1, last].wait_recv()
-        out = dot(hidden[...], w_out[...].reshape(n_tall * TILE, D)).astype(BF16)
-        made[rows] = out.reshape(room, WAYS, LANES)
-        exchange(made, back, take_send.at[0], take_recv, -1, group)
-    back[0:ROOM] = made[0:ROOM]
+        finish(0, group)
+        if group < 2:
+            onward(2, group, 3)
+    hops[2, 0, last].wait_recv()
+    hops[2, 1, last].wait_recv()
+    for group in range(groups):
+        finish(1, group)
+    back[:, 0:ROOM] = made[:, 0:ROOM]
     for copy in hops.values():
         copy.wait_send()
     whole_of(slots, n_wide - 1, give_send.at[0], give_recv.at[0]).wait_send()
-    for pair in range(groups // 2):
-        for group in (2 * pair, 2 * pair + 1):
-            whole_of(back, per - (group == 0), take_send.at[0], take_recv.at[group]).wait_recv()
-        part = dot(gather[pair], back[pair * span : pair * span + span].reshape(span, D))
-        if pair < groups // 2 - 1:
-            picked[...] = part if pair == 0 else picked[...] + part
+    for half in range(2):
+        cols = slice(half * TILE, half * TILE + TILE)
+        for pair in range(groups // 2):
+            for group in (2 * pair, 2 * pair + 1):
+                whole_of(
+                    back.at[half], per - (group == 0), take_send.at[half], take_recv.at[half, group]
+                ).wait_recv()
+            part = dot(gather[pair], back[half, pair * span : pair * span + span].reshape(span, TILE))
+            picked[:, cols] = part if pair == 0 else picked[:, cols] + part
     result_ref[...] = (
-        x1_ref[...].astype(F32) + gate[:, 0:1] * norm(picked[...] + part, moe_gain_ref[...])
+        x1_ref[...].astype(F32) + gate[:, 0:1] * norm(picked[...], moe_gain_ref[...])
     ).astype(BF16)
-    whole_of(made, n_wide - 1, take_send.at[0], take_recv.at[0]).wait_send()
+    for half in range(2):
+        whole_of(made.at[half], n_wide - 1, take_send.at[half], take_recv.at[half, 0]).wait_send()
 
 
 def body(
@@ -381,6 +405,7 @@
     hidden = expert_in.shape[2]
     rows = pltpu.VMEM((TOK, D), BF16)
     slot_buffer = pltpu.VMEM((experts * ROOM, WAYS, LANES), BF16)
+    half_buffer = pltpu.VMEM((2, experts * ROOM, WAYS // 2, LANES), BF16)
     DMA = pltpu.SemaphoreType.DMA
     ring_sem = DMA((2, n_tall // 2))
     out = pl.pallas_call(
@@ -399,14 +424,14 @@
             rows, rows, rows,
             pltpu.VMEM((experts * ROOM, TOK), BF16),
             pltpu.VMEM((4, TOK, experts * ROOM // 4), BF16),
-            slot_buffer, slot_buffer, slot_buffer, slot_buffer,
-            pltpu.VMEM((experts * ROOM // 8, n_tall * hidden), BF16),
+            slot_buffer, slot_buffer, half_buffer, half_buffer,
+            pltpu.VMEM((8, experts * ROOM // 8, n_tall * hidden), BF16),
             pltpu.VMEM((TOK, 128), F32),
             pltpu.VMEM((TOK, D), F32),
             pltpu.VMEM((n_tall, D, hidden), BF16),
-            pltpu.VMEM((n_tall, hidden, D), BF16),
-            DMA((5,)), pltpu.SemaphoreType.REGULAR, DMA((3,)), DMA((3,)), ring_sem, ring_sem, ring_sem, ring_sem,
-            DMA((1,)), DMA((8,)), DMA((1,)), DMA((8,)),
+            pltpu.VMEM((2, n_tall, hidden, TILE), BF16),
+            DMA((6,)), pltpu.SemaphoreType.REGULAR, DMA((3,)), DMA((3,)), ring_sem, ring_sem,
+            DMA((2, 2, n_tall // 2)), DMA((2, 2, n_tall // 2)), DMA((1,)), DMA((8,)), DMA((2,)), DMA((2, 8)),
         ],
         compiler_params=pltpu.CompilerParams(collective_id=0, has_side_effects=True, vmem_limit_bytes=62 << 20),
         name="block",

time: 87.8 us -> 89.3 us (1.017)
  the two profiles are of different devices: /device:TPU:2 before, /device:TPU:1 now
where the time goes in v5:
time: 89.3 us; the launch traced here: 89.1 us
  Pallas kernels  87.2 us (98%)
  local copies, waits for them, and re-layouts  1.92 us (2%)
    pallas_call x1, Pallas kernels, body(): pl.pallas_call(functools.partial(block_kernel, limits, experts), out_shap...  87.2 us
    unnamed x1, local copies, waits for them, and re-layouts  1.92 us

profile of v5, /device:TPU:1, one launch (start us, length us, event | category | flops | bytes accessed | tf_op | source)
XLA Modules:
  0.0 89.1 jit_solution(5928846496206530751)
XLA Ops:
  0.0 87.2 %block.1 = bf16[576,512]{1,0:T(8,128)(2,1)} custom-call(bf16[576,512]{1,0:T(8,128)(2,1)} %bitcast.10, bf16[512,1536]{1,0:T(8,128)(2,1)} %qkv_hbm.1, bf16[512,512]{1,0:T(8,128)(2,1)} %proj_hbm.1, f32[1,512]{1,0:T(1,128)} %bitcast.16, f32[16]{0:T(128)} %scale_ref.1, bf16[64,512]{1,0:T(8,128)(2,1)} %bitcast.13, bf16[512,256]{1,0:T(8,128)(2,1)} %bitcast.11, ...), custom_call_target="tpu_custom_call" | custom-call | tf_op jit(solution)/shard_map/block/pallas_call | solution.py:411
  87.2 1.9 %copy.13 = bf16[24,24,512]{2,1,0:T(8,128)(2,1)} copy(bf16[24,24,512]{2,1,0:T(8,128)(2,1)} %bitcast.9) | data formatting | bytes 1179648

commit v6 on v4

--- a/solution.py
+++ b/solution.py
@@ -303,7 +303,7 @@
     launch(1, 1, 1)
 
     def between(g):
-        for kind, way, step in (((0, 0, 1),), ((1, 0, 1),), ((0, 1, 1),), ((1, 1, 1), (0, 0, 2)))[g]:
+        for kind, way, step in (((0, 0, 1),), ((1, 0, 1),), (), ((0, 1, 1),))[g]:
             onward(kind, way, step)
 
     attend(q_ref, k_ref, k3_ref, v_ref, scale_ref, att_ref, between)
@@ -334,9 +334,11 @@
         slots[rows] = dot(scatter[rows, :], x1_ref[...]).astype(BF16).reshape(span, WAYS, LANES)
         for group in (2 * pair, 2 * pair + 1):
             exchange(slots, arrived, give_send.at[0], give_recv, 1, group)
-        if pair > 0:
-            onward(*((1, 0, 2), (0, 1, 2), (1, 1, 2))[pair - 1])
+        if pair % 2 == 0:
+            onward(*((1, 1, 1), (0, 0, 2))[pair // 2])
     arrived[0:ROOM] = slots[0:ROOM]
+    for kind, way, step in ((1, 0, 2), (0, 1, 2), (1, 1, 2)):
+        onward(kind, way, step)
     logit = jnp.sum(dot(x1_ref[...], router_ref[...], NT) * chosen, axis=-1, keepdims=True)
     gate[...] = jnp.broadcast_to(in_use * jax.nn.sigmoid(logit), gate.shape)
     onward(0, 0, 3)

time: 87.8 us -> 88.2 us (level)
  no operation moved by 1% of the time
where the time goes in v6:
time: 88.2 us; the launch traced here: 88 us
  Pallas kernels  86.1 us (98%)
  local copies, waits for them, and re-layouts  1.92 us (2%)
    pallas_call x1, Pallas kernels, body(): pl.pallas_call(functools.partial(block_kernel, limits, experts), out_shap...  86.1 us
    unnamed x1, local copies, waits for them, and re-layouts  1.92 us

profile of v6, /device:TPU:2, one launch (start us, length us, event | category | flops | bytes accessed | tf_op | source)
XLA Modules:
  0.0 88.0 jit_solution(17283586877957952211)
XLA Ops:
  0.0 86.1 %block.1 = bf16[576,512]{1,0:T(8,128)(2,1)} custom-call(bf16[576,512]{1,0:T(8,128)(2,1)} %bitcast.10, bf16[512,1536]{1,0:T(8,128)(2,1)} %qkv_hbm.1, bf16[512,512]{1,0:T(8,128)(2,1)} %proj_hbm.1, f32[1,512]{1,0:T(1,128)} %bitcast.16, f32[16]{0:T(128)} %scale_ref.1, bf16[64,512]{1,0:T(8,128)(2,1)} %bitcast.13, bf16[512,256]{1,0:T(8,128)(2,1)} %bitcast.11, ...), custom_call_target="tpu_custom_call" | custom-call | tf_op jit(solution)/shard_map/block/pallas_call | solution.py:388
  86.1 1.9 %copy.13 = bf16[24,24,512]{2,1,0:T(8,128)(2,1)} copy(bf16[24,24,512]{2,1,0:T(8,128)(2,1)} %bitcast.9) | data formatting | bytes 1179648
